TPU v7x, 32 devices: a whole 2x2x4 slice. The times are simulated.
32 devices in a mesh: section: 2 (over core), batch: 16 (over z, y, x).
Axes of the slice: x: 2, y: 2, z: 4, core: 2. Of those that a mesh axis runs over, the one named last changes fastest.
Arguments:
- frames: bfloat16 [4, 84, 84, 4096], P(None, None, None, 'batch'), may hold values from -6 to 6
- destination: int32 [4096], P('batch'), may hold values from 0 to 15, as said below
- options: int32 [3, 4096], P(None, 'batch'), may hold values from 0 to 17
- depth: int32 [4096], P('batch'), may hold values from 1 to 3
- targets: float32 [3, 3, 4096], P(None, None, 'batch'), may hold values from -6 to 6
- conv_one: bfloat16 [256, 16], replicated, may hold values from -0.375 to 0.375
- bias_one: float32 [16], replicated, may hold values from -3 to 3
- conv_two: bfloat16 [256, 32], replicated, may hold values from -0.375 to 0.375
- bias_two: float32 [32], replicated, may hold values from -3 to 3
- linear_w: bfloat16 [2592, 128], replicated, may hold values from -0.125 to 0.125
- linear_b: float32 [128], replicated, may hold values from -3 to 3
- branch_w: bfloat16 [18, 128, 128], replicated, may hold values from -0.5 to 0.5
- branch_b: float32 [18, 128], replicated, may hold values from -3 to 3
- head_w: bfloat16 [128, 2], replicated, may hold values from -0.5 to 0.5
- head_b: float32 [2], replicated, may hold values from -3 to 3
- value_w: bfloat16 [128, 128], replicated, may hold values from -0.5 to 0.5
- value_b: float32 [128], replicated, may hold values from -3 to 3
- out_w: bfloat16 [128, 1], replicated, may hold values from -0.5 to 0.5
- out_b: float32 [1], replicated, may hold values from -3 to 3
Outputs:
- loss: float32 [], replicated
- frames_grad: float32 [4, 84, 84, 4096], P('section', None, None, 'batch')
- conv_one_grad: float32 [256, 16], replicated
- bias_one_grad: float32 [16], replicated
- conv_two_grad: float32 [256, 32], replicated
- bias_two_grad: float32 [32], replicated
- linear_w_grad: float32 [2592, 128], replicated
- linear_b_grad: float32 [128], replicated
- branch_w_grad: float32 [18, 128, 128], replicated
- branch_b_grad: float32 [18, 128], replicated
- head_w_grad: float32 [128, 2], replicated
- head_b_grad: float32 [2], replicated
- value_w_grad: float32 [128, 128], replicated
- value_b_grad: float32 [128], replicated
- out_w_grad: float32 [128, 1], replicated
- out_b_grad: float32 [1], replicated
Inputs may be any that keep to these rules, and one draw needn't show every extreme that they name: `destination`: among the 256 frames of each batch index, every planner index appears exactly 16 times.
All inputs are finite; a program needn't handle non-finite values.
Results may differ from a plain program's by a relative error of at most 0.013.
Values may be sent and summed in bfloat16 or wider, within the bound.
No kernel may reach another device: no remote copies, remote signals or barrier semaphores. Data moves between devices by JAX's collectives and lax.ppermute only.
A program may use at most 256 MiB of HBM per device.

v0:
```python
import functools
import math

import jax
import jax.numpy as jnp
from jax import lax
from jax.experimental import pallas as pl
from jax.experimental.pallas import tpu as pltpu
from jax.sharding import PartitionSpec as P

BF16 = jnp.bfloat16
F32 = jnp.float32
EXACT = lax.Precision.HIGHEST
LANES = 128
VMEM_BYTES = 32 * 1024 * 1024
TILE = 16
REACH = 5
STEP = 3
COLS = 12
NEAR = 4
AT_VB, AT_OW, AT_HW, AT_LB, AT_SCALARS, AT_B1, AT_B2, AT_DEST = (
    slice(18, 19),
    slice(19, 20),
    slice(20, 22),
    slice(22, 23),
    slice(23, 24),
    slice(24, 25),
    slice(25, 26),
    26,
)
TABLE = 32
CUBE = 8
DRAW = 4
SHORT = 16


def dot(a, b, precision=None):
    return jnp.dot(a, b, preferred_element_type=F32, precision=precision)


def dot_rows(a, b, precision=None):
    return lax.dot_general(
        a, b, (((0,), (0,)), ((), ())), preferred_element_type=F32, precision=precision
    )


def dot_lanes(a, b, precision=None):
    return lax.dot_general(
        a, b, (((1,), (1,)), ((), ())), preferred_element_type=F32, precision=precision
    )


def iota(shape, axis):
    return lax.broadcasted_iota(jnp.int32, shape, axis)


def column(row):
    n = row.shape[1]
    wide = jnp.broadcast_to(row, (n, n))
    return jnp.sum(jnp.where(iota((n, n), 0) == iota((n, n), 1), wide, 0.0), axis=1, keepdims=True)


def row_of(col):
    n = col.shape[0]
    wide = jnp.broadcast_to(col, (n, n))
    return jnp.sum(jnp.where(iota((n, n), 0) == iota((n, n), 1), wide, 0.0), axis=0, keepdims=True)


def soft(x):
    t = jnp.tanh(0.5 * x)
    return jnp.maximum(x, 0.0) - jnp.log(0.5 + 0.5 * jnp.abs(t)), 0.5 + 0.5 * t


def silu_pair(y):
    t = jnp.tanh(y)
    m = y * t
    return y + m, (1.0 + t) + (y - m * t)


def pixel_order(w1t):
    tap, pix = iota((256, 256), 0), iota((256, 256), 1)
    moves = ((tap >> 6) == (pix & 3)) & ((tap & 63) == (pix >> 2))
    return dot(w1t, moves.astype(F32).astype(BF16))


def frame_copies(section, far, here, sems):
    lanes = pl.ds(pl.multiple_of(section[0] * LANES, LANES), LANES)
    size = 4 * STEP

    def copy(g):
        rows = pl.ds(pl.multiple_of(g * size, size), size)
        return pltpu.make_async_copy(far.at[rows, :, :, lanes], here.at[rows], sems.at[g])

    return copy


def tile_rows(frames, row, j, cols):
    img, _, channels, _ = frames.shape
    flat = frames.reshape(img, img * channels, LANES)
    size = cols * channels
    end = min((j + 1) * size, img * channels)
    part = flat[pl.ds(row, 4), j * size : end, :]
    return part.reshape(4 * (end - j * size), LANES)


def encode_kernel(
    section,
    frames_far,
    w1t,
    w2t,
    lw_far,
    table,
    h1_far,
    s1_far,
    s2_far,
    h2,
    enc,
    s3,
    frames,
    lw,
    h1,
    s1,
    s2,
    band,
    edge,
    band2,
    bias1,
    bias2,
    held,
    held2,
    sems,
):
    blocks, side = h1.shape[:2]
    steps = blocks // STEP
    tiles = frames.shape[1] // TILE
    k1, k2 = w1t.shape[0], w2t.shape[0]
    reach_rows = REACH * k1
    arrives = frame_copies(section, frames_far, frames, sems.at[0])
    for g in range(steps):
        arrives(g).start()
    last_copies = [
        pltpu.make_async_copy(lw_far, lw, sems.at[3, 0]),
        pltpu.make_async_copy(s2, s2_far, sems.at[3, 1]),
    ]
    last_copies[0].start()

    def leaves(g):
        rows = pl.ds(g * STEP, STEP)
        return [
            pltpu.make_async_copy(h1.at[rows], h1_far.at[rows], sems.at[1, g]),
            pltpu.make_async_copy(s1.at[rows], s1_far.at[rows], sems.at[2, g]),
        ]

    inner = side // 2 - 1
    row_len = inner * k2
    two = 2 * k2 * 3

    def prepare():
        taps = pixel_order(w1t[...])
        edges = []
        for half in range(2):
            lines = [taps[:, 32 * (4 * half + u) : 32 * (4 * half + u + 1)] for u in range(4)]
            for place in range(REACH):
                pieces = []
                for line in lines:
                    start = 16 * (place - 1)
                    cut = line[:, max(0, -start) : min(32, 64 - start)]
                    start = max(start, 0)
                    pieces += [jnp.zeros((k1, start), F32)] if start else []
                    pieces.append(cut)
                    rest = 64 - start - cut.shape[1]
                    pieces += [jnp.zeros((k1, rest), F32)] if rest else []
                at = half * reach_rows + place * k1
                band[at : at + k1, :] = jnp.concatenate(pieces, axis=1).astype(BF16)
            edges.append(jnp.concatenate([line[:, 16:] for line in lines], axis=1))
        edge[...] = jnp.concatenate(edges, axis=0).astype(BF16)
        tap, pix = iota((256, LANES), 0), iota((256, LANES), 1)
        for half in range(2):
            for place in range(3):
                hit = (
                    ((tap & 15) == (pix & 15))
                    & ((tap >> 6) == (pix >> 6) + 2 * half)
                    & (((tap >> 4) & 3) == ((pix >> 4) & 3) + 2 - 2 * place)
                )
                at = (half * 3 + place) * k2
                taps = dot(w2t[...], hit.astype(F32).astype(BF16))
                band2[at : at + k2, :] = taps.astype(BF16)
        bias1[...] = jnp.broadcast_to(column(table[AT_B1, 0:k1]), bias1.shape)
        bias2[...] = jnp.broadcast_to(column(table[AT_B2, 0:k2]), bias2.shape)
        held[...] = jnp.zeros_like(held)
        held2[...] = jnp.zeros_like(held2)
        h1[...] = jnp.zeros_like(h1)

    def added(sums, x, value):
        sums[x] = sums[x] + value if x in sums else value

    def second_matmul(b):
        tiles = [
            h1[pl.ds(2 * b + 1, 2), 4 * j : 4 * j + 4].reshape(LANES, LANES)
            for j in range(side // 4)
        ]
        return dot(band2[...], jnp.concatenate(tiles, axis=1))

    def second_rows(b, got):
        low, high = {}, {}
        for j in range(side // 4):
            for place in range(3):
                x = 2 * j - 1 + place
                if 0 <= x < inner:
                    span = slice(j * LANES, (j + 1) * LANES)
                    at = place * k2
                    added(low, x, got[at : at + k2, span])
                    added(high, x, got[two // 2 + at : two // 2 + at + k2, span])
        row = jnp.maximum(b - 1, 0) * row_len
        for x in range(inner):
            value, slope = soft(held2[x] + high[x] + bias2[...])
            held2[x] = low[x]
            at = pl.ds(pl.multiple_of(row + x * k2, k2), k2)
            h2[at, :] = value.astype(BF16)
            s2[at, :] = slope.astype(BF16)

    def one_step(g, carry):
        def row(r):
            return pl.multiple_of(4 * (STEP * g + r), 4)

        arrives(g).wait()
        lows, highs = [{} for _ in range(STEP)], [{} for _ in range(STEP)]

        def place_tile(r, j, got):
            for place in range(REACH):
                x = 4 * j - 1 + place
                if 0 <= x < side:
                    at = place * k1
                    added(lows[r], x, got[at : at + k1])
                    added(highs[r], x, got[reach_rows + at : reach_rows + at + k1])

        def finish(r, xs):
            for x in xs:
                value, slope = soft(held[x] + highs[r][x] + bias1[...])
                held[x] = lows[r][x]
                h1[STEP * g + r, x] = value.astype(BF16)
                s1[STEP * g + r, x] = slope.astype(BF16)

        pair = jnp.maximum(g - 1, 0)
        units = [(lambda: second_matmul(pair), lambda got: second_rows(pair, got))]

        def edges():
            parts = [tile_rows(frames, row(r), tiles, TILE) for r in range(STEP)]
            return dot(edge[...], jnp.concatenate(parts, axis=1))

        def place_edges(got):
            for r in range(STEP):
                added(lows[r], side - 1, got[:k1, r * LANES : (r + 1) * LANES])
                added(highs[r], side - 1, got[k1:, r * LANES : (r + 1) * LANES])

        units.append((edges, place_edges))

        def full(spots):
            parts = [tile_rows(frames, row(r), j, TILE) for r, j in spots]
            return dot(band[...], jnp.concatenate(parts, axis=1))

        def place_full(got, spots, ready):
            for i, (r, j) in enumerate(spots):
                place_tile(r, j, got[:, i * LANES : (i + 1) * LANES])
            if ready:
                finish(*ready)

        for r in range(STEP):
            if r % 2 == 0:
                spots = [(k, tiles - 1) for k in (r, r + 1) if k < STEP]
                units.append(
                    (
                        functools.partial(full, spots),
                        functools.partial(place_full, spots=spots, ready=None),
                    )
                )
            done = 0
            for j in range(0, tiles - 1, 2):
                spots = [(r, j), (r, j + 1)]
                ready = side if j + 2 == tiles - 1 else 4 * j + 7
                units.append(
                    (
                        functools.partial(full, spots),
                        functools.partial(place_full, spots=spots, ready=(r, range(done, ready))),
                    )
                )
                done = ready
        waiting = None
        for issue, take in units:
            got = issue()
            if waiting is not None:
                waiting[0](waiting[1])
            waiting = (take, got)
        waiting[0](waiting[1])
        for copy in leaves(g):
            copy.start()
        return carry

    prepare()
    lax.fori_loop(0, steps, one_step, 0)
    for b in range(steps - 1, side // 2):
        second_rows(b, second_matmul(b))
    for copy in last_copies[1:]:
        copy.start()
    last_copies[0].wait()
    value, slope = soft(dot_rows(lw[...], h2[...]) + column(table[AT_LB, :]))
    enc[...] = value.astype(BF16)
    s3[...] = slope
    for g in range(steps):
        for copy in leaves(g):
            copy.wait()
    for copy in last_copies[1:]:
        copy.wait()


def three_parts(row):
    high = row.astype(BF16).astype(F32)
    middle = (row - high).astype(BF16).astype(F32)
    return jnp.concatenate([high, middle, row - high - middle], axis=0)


def with_ones(value):
    return jnp.concatenate([value, ones_rows(value.shape[1])], axis=0)


def ones_rows(lanes):
    return (iota((16, lanes), 0) < 3).astype(F32).astype(BF16)


def plan_kernel(
    section,
    slots,
    enc,
    s3,
    h2,
    branch_far,
    value_w,
    table,
    keep,
    send_one,
    send_two,
    small,
    g3,
    parts,
    bwt,
    vht,
    vhw,
    ow,
    mine,
    pre,
    dbr,
    dval,
    low,
    hid,
    gb,
    branch_w,
    sem,
    *,
    per_pair,
    depth,
):
    width = enc.shape[0]
    options = branch_w.shape[0]
    pairs = options // 2
    two = 2 * width
    sec = section[0]
    branch_copy = pltpu.make_async_copy(branch_far, branch_w, sem)
    branch_copy.start()

    count = slots.shape[0]
    dest = jnp.concatenate(
        [table[AT_DEST + k : AT_DEST + k + 1, :] for k in range(count // LANES)], axis=1
    )
    own = jnp.where(sec == 0, dest[:, :LANES], dest[:, LANES:])
    others = jnp.transpose(jnp.broadcast_to(dest, (LANES, count)))
    index = iota((count, LANES), 1) + sec * LANES
    earlier = (others == own) & (iota((count, LANES), 0) < index)
    rank = jnp.sum(earlier.astype(F32), axis=0, keepdims=True)
    bucket = own * float(per_pair) + rank
    chosen = (iota((count, LANES), 0).astype(F32) == bucket).astype(F32).astype(BF16)
    numbers = slots[:, : mine.shape[0]]
    high = numbers.astype(BF16)
    middle = (numbers - high.astype(F32)).astype(BF16)
    rest = (numbers - high.astype(F32) - middle.astype(F32)).astype(BF16)
    mine[...] = sum(dot_rows(v, chosen) for v in (rest, middle, high))

    pad = jnp.zeros((13, width), F32)
    branch_copy.wait()
    for o in range(options):
        rows = [branch_w[o].astype(F32), three_parts(table[o : o + 1, :]), pad]
        bwt[o * width : (o + 1) * width, :] = jnp.transpose(
            0.5 * jnp.concatenate(rows, axis=0)
        ).astype(BF16)
    scalars = table[AT_SCALARS, :]
    head_w = table[AT_HW, :]
    rows = [value_w[...].astype(F32), three_parts(table[AT_VB, :]), pad]
    vht[0:width, :] = jnp.transpose(0.5 * jnp.concatenate(rows, axis=0)).astype(BF16)
    vht[width:, :] = jnp.zeros((16, width + 16), BF16)
    lane = iota((1, 16), 1)
    for k in range(2):
        bias = three_parts(jnp.broadcast_to(scalars[:, 1 + k : 2 + k], (1, 16)))
        bias = sum(jnp.where(lane == j, bias[j : j + 1], 0.0) for j in range(3))
        vht[width + k : width + k + 1, 0:width] = head_w[k : k + 1].astype(BF16)
        vht[width + k : width + k + 1, width:] = bias.astype(BF16)
    vhw[:, 0:width] = (0.5 * value_w[...].astype(F32)).astype(BF16)
    vhw[:, width:] = jnp.transpose(
        0.5 * jnp.concatenate([head_w, jnp.zeros((14, width), F32)], axis=0)
    ).astype(BF16)
    ow[...] = jnp.broadcast_to(column(table[AT_OW, :]), (width, LANES))
    wide_ow = jnp.concatenate([ow[...], ow[...]], axis=1)
    half_ow = 0.5 * wide_ow

    labels = iota((options, LANES), 0).astype(F32)
    state = enc[...].astype(F32)
    rounded_all, saved = [], []
    group = 3
    for level in range(depth):
        picked = labels == mine[level : level + 1, :]
        rounded = state.astype(BF16)
        rounded_all.append(rounded)
        met = with_ones(rounded)

        def branches(first):
            at = slice(first * two, (first + group) * two)
            pre[at, :] = dot(bwt[at, :], met)

        branches(0)
        following = state
        reward, discount, value = [], [], []

        def value_part(t, got):
            act, slope = silu_pair(got[:width])
            dval[level, t] = slope
            hidden = act.astype(BF16)
            hid[level, t] = hidden
            worth = jnp.sum(hidden.astype(F32) * wide_ow, axis=0, keepdims=True)
            for k in range(2):
                span = slice(k * LANES, (k + 1) * LANES)
                value.append(worth[:, span])
                reward.append(got[width : width + 1, span])
                discount.append(got[width + 1 : width + 2, span])

        waiting = None
        for first in range(0, pairs, group):
            if first + group < pairs:
                branches(first + group)
            boths = []
            for t in range(first, first + group):
                at = slice(t * two, (t + 1) * two)
                act, slope = silu_pair(pre[at, :])
                dbr[level, at, :] = slope
                left = state + act[:width]
                right = state + act[width:]
                following = jnp.where(picked[2 * t : 2 * t + 1], left, following)
                following = jnp.where(picked[2 * t + 1 : 2 * t + 2], right, following)
                both = with_ones(
                    jnp.concatenate([left.astype(BF16), right.astype(BF16)], axis=1)
                )
                low[level, t] = both
                boths.append(both)
            got = dot(vht[...], jnp.concatenate(boths, axis=1))
            if waiting is not None:
                for k in range(group):
                    value_part(waiting[0] + k, waiting[1][:, k * two : (k + 1) * two])
            waiting = (first, got)
        for k in range(group):
            value_part(waiting[0] + k, waiting[1][:, k * two : (k + 1) * two])
        reward = jnp.concatenate(reward, axis=0)
        discount = jax.nn.sigmoid(jnp.concatenate(discount, axis=0))
        value = jnp.concatenate(value, axis=0) + scalars[:, 3:4]
        quality = reward + discount * value
        top = jnp.max(quality, axis=0, keepdims=True)
        shifted = jnp.exp(quality - top)
        total = jnp.sum(shifted, axis=0, keepdims=True)
        live = (mine[depth : depth + 1, :] > level).astype(F32)
        chosen = picked.astype(F32)

        def target(kind):
            at = depth + 1 + kind * depth + level
            return mine[at : at + 1, :]

        reward_gap = live * (jnp.sum(chosen * reward, axis=0, keepdims=True) - target(0))
        discount_gap = live * (jnp.sum(chosen * discount, axis=0, keepdims=True) - target(1))
        plan_gap = live * (top + jnp.log(total) - target(2))
        grad_quality = plan_gap * (shifted / total)
        head_two = (chosen * discount_gap + grad_quality * value) * discount * (1.0 - discount)
        saved.append(
            (
                picked,
                (chosen * reward_gap + grad_quality).astype(BF16).astype(F32),
                head_two.astype(BF16).astype(F32),
                (grad_quality * discount).astype(BF16).astype(F32),
                reward_gap * reward_gap + discount_gap * discount_gap + plan_gap * plan_gap,
            )
        )
        state = following

    out_sum = jnp.zeros((16, width), F32)
    value_sum = jnp.zeros((width + 16, width + 16), F32)
    grad_next = None
    line = iota((16, two), 0)
    for level in reversed(range(depth)):
        picked, head_one, head_two, grad_value, _ = saved[level]
        upward = jnp.zeros((width, LANES), F32)

        def branch_part(t, moved):
            at = slice(t * two, (t + 1) * two)
            left, right = moved[:, :LANES], moved[:, LANES:]
            if grad_next is not None:
                left = left + jnp.where(picked[2 * t : 2 * t + 1], grad_next, 0.0)
                right = right + jnp.where(picked[2 * t + 1 : 2 * t + 2], grad_next, 0.0)
            grad_branch = jnp.concatenate([left, right], axis=0) * dbr[level, at, :]
            grad_branch = grad_branch.astype(BF16)
            gb[level, at, :] = grad_branch
            return left + right

        def group_part(first, moved):
            parts = [
                branch_part(first + k, moved[:, k * two : (k + 1) * two]) for k in range(group)
            ]
            at = slice(first * two, (first + group) * two)
            weights = [branch_w[o] for o in range(2 * first, 2 * (first + group))]
            return sum(parts), dot(jnp.concatenate(weights, axis=1), gb[level, at, :])

        waiting = None
        for first in range(0, pairs, group):
            stack = []
            for t in range(first, first + group):

                def across(rows):
                    return jnp.concatenate(
                        [rows[2 * t : 2 * t + 1], rows[2 * t + 1 : 2 * t + 2]], axis=1
                    )

                worth = across(grad_value)
                grad_pre = (worth * half_ow * dval[level, t]).astype(BF16)
                heads = jnp.where(line == 0, across(head_one), 0.0)
                heads = jnp.where(line == 1, across(head_two), heads)
                heads = jnp.where(line == 2, worth, heads)
                heads = heads.astype(BF16)
                out_sum = out_sum + dot_lanes(heads, hid[level, t])
                stack.append(jnp.concatenate([grad_pre, heads], axis=0))
            stack = jnp.concatenate(stack, axis=1)
            moved = dot(vhw[...], stack)
            if waiting is not None:
                one, other = group_part(*waiting)
                upward = upward + (one + 0.5 * other)
            waiting = (first, moved)
            lows = jnp.concatenate([low[level, first + k] for k in range(group)], axis=1)
            value_sum = value_sum + dot_lanes(stack, lows)
        one, other = group_part(*waiting)
        grad_next = upward + (one + 0.5 * other)

    linear_rows = h2.shape[0]
    half = (linear_rows + options * width + width) // 2
    rest = linear_rows - half
    rounded = with_ones(jnp.concatenate(rounded_all, axis=1))
    small[...] = jnp.zeros_like(small)
    if half < keep.shape[0]:
        for k in range(2):
            parts[k, half:, :] = jnp.zeros((keep.shape[0] - half, LANES), BF16)
    for t in range(pairs):
        at = slice(t * two, (t + 1) * two)
        grads = jnp.concatenate([gb[level, at, :] for level in range(depth)], axis=1)
        got = dot_lanes(rounded, grads)
        for k in range(2):
            o = 2 * t + k
            span = slice(k * width, (k + 1) * width)
            rows = slice(rest + o * width, rest + (o + 1) * width)
            parts[1 - sec, rows, :] = got[:width, span].astype(BF16)
            small[o : o + 1, :] = got[width : width + 1, span]
    after = rest + options * width
    parts[1 - sec, after : after + width, :] = jnp.transpose(value_sum[:width, :width]).astype(BF16)

    grad_three = ((2.0 * grad_next).astype(BF16).astype(F32) * s3[...]).astype(BF16)
    g3[...] = grad_three
    chunk = linear_rows // 9
    for i in range(8):
        at = slice(i * chunk, (i + 1) * chunk)
        parts[sec, at, :] = dot_lanes(h2[at, :], grad_three).astype(BF16)
    last = dot_lanes(h2[8 * chunk :, :], grad_three).astype(BF16)
    parts[sec, 8 * chunk : half, :] = last[: half - 8 * chunk]
    parts[1 - sec, 0:rest, :] = last[half - 8 * chunk :]
    keep[...] = parts[0]
    send_one[...] = parts[1, : send_one.shape[0]]
    send_two[...] = parts[1, send_one.shape[0] :]

    small[AT_VB, :] = row_of(value_sum[:width, width : width + 1])
    small[AT_OW, :] = out_sum[2:3]
    small[AT_HW, :] = value_sum[width : width + 2, :width]
    small[AT_LB, :] = row_of(jnp.sum(grad_three.astype(F32), axis=1, keepdims=True))
    loss = 0.5 * jnp.sum(sum(kept[4] for kept in saved), axis=1, keepdims=True)
    ends = [loss] + [value_sum[width + k : width + k + 1, width : width + 1] for k in range(3)]
    lane = iota((1, LANES), 1)
    line = jnp.zeros((1, LANES), F32)
    for k, end in enumerate(ends):
        line = jnp.where(lane == k, end, line)
    small[AT_SCALARS, :] = line


def back_kernel(g3, lw, s2, s1, h1, w2t, g1, c2, sums, t2, g2):
    side, k1 = s1.shape[1], s1.shape[2]
    k2 = w2t.shape[0]
    inner = side // 2 - 1
    row_len = inner * k2
    tap, pix = iota((LANES, 256), 1), iota((LANES, 256), 0)
    for yrel in range(2):
        for p in range(3):
            hit = (
                ((tap & 15) == (pix & 15))
                & ((tap >> 6) == (pix >> 6) + 2 * (1 - yrel))
                & (((tap >> 4) & 3) == ((pix >> 4) & 3) + 2 - 2 * p)
            )
            at = (yrel * 3 + p) * k2
            t2[:, at : at + k2] = dot_lanes(hit.astype(F32).astype(BF16), w2t[...]).astype(BF16)
    g2[0] = jnp.zeros(g2.shape[1:], BF16)
    g2[inner + 1] = jnp.zeros(g2.shape[1:], BF16)
    g1[0] = jnp.zeros(g1.shape[1:], BF16)
    g1[side + 1] = jnp.zeros(g1.shape[1:], BF16)
    zero = jnp.zeros((k2, LANES), BF16)
    total_one = jnp.zeros((k1, LANES), F32)
    total_two = jnp.zeros((k2, LANES), F32)
    for y in range(inner):
        at = slice(y * row_len, (y + 1) * row_len)
        grad = dot(lw[at, :], g3[...]) * s2[at, :].astype(F32)
        grad = grad.astype(BF16).reshape(inner, k2, LANES)
        g2[y + 1] = grad
        total_two = total_two + jnp.sum(grad.astype(F32), axis=0)
    reach, cols = 5, 8
    total = jnp.zeros((2 * reach * k2, 2 * cols * k1), F32)
    grads, tiles = [], []
    for b in range(side // 2):
        cut = []
        for j in range(side // 4):
            pieces = []
            for yrel in range(2):
                for p in range(3):
                    x = 2 * j - 1 + p
                    pieces.append(g2[b + yrel, x] if 0 <= x < inner else zero)
            cut.append(jnp.concatenate(pieces, axis=0))
        got = dot(t2[...], jnp.concatenate(cut, axis=1))
        for u in range(2):
            for j in range(side // 4):
                part = got[u * 64 : (u + 1) * 64, j * LANES : (j + 1) * LANES]
                slope = s1[2 * b + u + 1, 4 * j : 4 * j + 4].astype(F32)
                grad = (part.reshape(4, k1, LANES) * slope).astype(BF16)
                g1[2 * b + u + 1, 4 * j : 4 * j + 4] = grad
                total_one = total_one + jnp.sum(grad.astype(F32), axis=0)
        for j in range(-(-side // cols)):
            end = min((j + 1) * cols, side)
            tile = h1[2 * b + 1 : 2 * b + 3, j * cols : end]
            if end < (j + 1) * cols:
                rest = jnp.zeros((2, (j + 1) * cols - end, k1, LANES), BF16)
                tile = jnp.concatenate([tile, rest], axis=1)
            tiles.append(tile.reshape(2 * cols * k1, LANES))
            pieces = []
            for half in range(2):
                for p in range(reach):
                    x = 4 * j - 1 + p
                    pieces.append(g2[b + 1 - half, x] if 0 <= x < inner else zero)
            grads.append(jnp.concatenate(pieces, axis=0))
        if b % 2:
            total = total + dot_lanes(
                jnp.concatenate(grads, axis=1), jnp.concatenate(tiles, axis=1)
            )
            grads, tiles = [], []
    line = 4 * k1
    for half in range(2):
        for u in range(2):
            tap_row = jnp.zeros((k2, line), F32)
            for p in range(reach):
                at = (half * reach + p) * k2
                part = total[at : at + k2, u * 2 * line : (u + 1) * 2 * line]
                start = 2 * k1 * (p - 1)
                piece = part[:, max(start, 0) : min(start + line, 2 * line)]
                if start < 0:
                    piece = jnp.concatenate([jnp.zeros((k2, -start), F32), piece], axis=1)
                if start + line > 2 * line:
                    rest = jnp.zeros((k2, start - line), F32)
                    piece = jnp.concatenate([piece, rest], axis=1)
                tap_row = tap_row + piece
            at = (2 * half + u) * line
            c2[:, at : at + line] = tap_row
    sums[...] = jnp.zeros_like(sums)
    sums[0:1, 0:k1] = row_of(jnp.sum(total_one, axis=1, keepdims=True))
    sums[1:2, 0:k2] = row_of(jnp.sum(total_two, axis=1, keepdims=True))


def pixel_band(sec, w1t, channels):
    k1 = w1t.shape[0]
    rows = 64 * channels
    row, tap = iota((rows, 256), 0), iota((rows, 256), 1)
    moves = ((tap >> 6) == row % channels + sec * channels) & ((tap & 63) == row // channels)
    taps = dot_lanes(moves.astype(F32).astype(BF16), w1t)
    line, span = COLS * channels, 8 * channels
    blocks = {}
    for half in range(2):
        for p in range(NEAR):
            pieces = []
            for u in range(4):
                at = (4 * half + u) * span
                start = 4 * (p - 1) * channels
                cut = taps[at + max(0, -start) : at + min(span, line - start)]
                start = max(start, 0)
                pieces += [jnp.zeros((start, k1), F32)] if start else []
                pieces.append(cut)
                rest = line - start - cut.shape[0]
                pieces += [jnp.zeros((rest, k1), F32)] if rest else []
            blocks[half, p] = jnp.concatenate(pieces, axis=0)
    zero = jnp.zeros((4 * line, k1), F32)
    lines = []
    for r in range(STEP):
        cols = [
            blocks.get((r + 1 - yrel, p), zero) for yrel in range(STEP + 1) for p in range(NEAR)
        ]
        lines.append(jnp.concatenate(cols, axis=1))
    return jnp.concatenate(lines, axis=0).astype(BF16)


def first_kernel(
    section,
    frames_far,
    g1,
    w1t,
    other_far,
    after,
    c1,
    out,
    band,
    frames,
    acc,
    other,
    held,
    sems,
    draw_sems,
    *,
    draw,
):
    side, k1 = g1.shape[1], g1.shape[2]
    img, _, channels, _ = frames.shape
    steps = img // 4 // STEP
    arrives = frame_copies(section, frames_far, frames, sems)
    for g in range(steps):
        arrives(g).start()
    other_copy = pltpu.make_async_copy(
        other_far.at[0 : STEP * draw + 1], other, sems.at[steps]
    )
    other_copy.start()
    acc[...] = jnp.zeros_like(acc)
    zero = jnp.zeros((k1, LANES), BF16)

    def one_step(g, carry):
        arrives(g).wait()
        pixels, grads = [], []
        for j in range(img // COLS):
            rows = [pl.multiple_of(4 * (STEP * g + r), 4) for r in range(STEP)]
            pixels.append(
                jnp.concatenate([tile_rows(frames, row, j, COLS) for row in rows], axis=0)
            )
            pieces = []
            for yrel in range(STEP + 1):
                for p in range(NEAR):
                    x = 3 * j - 1 + p
                    pieces.append(g1[STEP * g + yrel, x] if 0 <= x < side else zero)
            grads.append(jnp.concatenate(pieces, axis=0))
        acc[...] += dot_lanes(jnp.concatenate(pixels, axis=1), jnp.concatenate(grads, axis=1))
        return carry

    lax.fori_loop(0, steps, one_step, 0)
    band[...] = pixel_band(section[0], w1t[...], out.shape[2])
    other_copy.wait()
    finish = draw_steps(section, band, g1, 0, other, 0, out, held, draw_sems, 0, draw)
    fold_first(acc, c1, channels, k1)
    finish()


def fold_first(acc, c1, channels, k1):
    line = COLS * channels
    step = 4 * channels
    taps = []
    for half in range(2):
        total = sum(
            acc[r * 4 * line : (r + 1) * 4 * line, :][
                :, (r + 1 - half) * NEAR * k1 : (r + 2 - half) * NEAR * k1
            ]
            for r in range(STEP)
        )
        for u in range(4):
            part = total[u * line : (u + 1) * line]
            cols = [part[:, p * k1 : (p + 1) * k1] for p in range(NEAR)]
            taps.append(cols[1][0:step] + cols[2][step : 2 * step] + cols[3][2 * step :])
            taps.append(cols[0][0:step] + cols[1][step : 2 * step] + cols[2][2 * step :])
    row, col = iota((256, 256), 0), iota((256, 256), 1)
    moves = ((row & 3) == (col >> 6)) & ((row >> 2) == (col & 63))
    grad = dot_rows(jnp.concatenate(taps, axis=0), moves.astype(F32), EXACT)
    for half in range(2):
        c1[half * k1 : (half + 1) * k1, :] = grad[:, half * LANES : (half + 1) * LANES].astype(BF16)


def draw_steps(section, band, mine, mine_at, other, other_at, out, held, sems, start, steps):
    side, k1 = mine.shape[1], mine.shape[2]
    img, channels = out.shape[1], out.shape[2]
    sec = section[0]
    line = COLS * channels
    flat = held.reshape(2, 2, 4 * STEP, img * channels, LANES)

    def writes(g):
        rows = slice(4 * STEP * (start + g), 4 * STEP * (start + g + 1))
        places = (sec * LANES, (1 - sec) * LANES)
        return [
            pltpu.make_async_copy(
                held.at[g % 2, k],
                out.at[rows, :, :, pl.ds(pl.multiple_of(places[k], LANES), LANES)],
                sems.at[g % 2, k],
            )
            for k in range(2)
        ]

    zero = jnp.zeros((k1, 2 * LANES), BF16)
    for g in range(steps):
        if g >= 2:
            for copy in writes(g - 2):
                copy.wait()
        for j in range(img // COLS):
            pieces = []
            for yrel in range(STEP + 1):
                for p in range(NEAR):
                    x, y = 3 * j - 1 + p, STEP * (start + g) + yrel
                    if 0 <= x < side:
                        pair = [mine[y - mine_at, x], other[y - other_at, x]]
                        pieces.append(jnp.concatenate(pair, axis=1))
                    else:
                        pieces.append(zero)
            got = dot(band[...], jnp.concatenate(pieces, axis=0))
            for k in range(4 * STEP):
                at = slice(k * line, (k + 1) * line)
                span = slice(j * line, (j + 1) * line)
                flat[g % 2, 0, k, span, :] = got[at, :LANES]
                flat[g % 2, 1, k, span, :] = got[at, LANES:]
        for copy in writes(g):
            copy.start()

    def finish():
        for g in range(max(steps - 2, 0), steps):
            for copy in writes(g):
                copy.wait()

    return finish


def pixels_kernel(section, band, mine, other_far, after, done, out, token, held, other, sems, *, start):
    steps = other.shape[0] // STEP
    fetch = pltpu.make_async_copy(
        other_far.at[STEP * start : STEP * (start + steps) + 1], other, sems.at[2, 0]
    )
    fetch.start()
    token[...] = jnp.zeros_like(token)
    fetch.wait()
    draw_steps(
        section, band, mine, 0, other, STEP * start, out, held, sems, start, steps
    )()


def two_parts(value):
    high = value.astype(BF16).astype(F32)
    return jnp.concatenate([high, value - high], axis=0).astype(BF16)


def one_part(pair):
    rows = pair.shape[0] // 2
    pair = pair.astype(F32)
    return pair[:rows] + pair[rows:]


def merge_kernel(keep, recv_one, recv_two, small, c2, sums, out_far, lines, out, sems):
    members = out.shape[0]
    size = keep.shape[0] // members
    lines[...] = small[...]
    lines[AT_B1, :] = sums[0:1, :]
    lines[AT_B2, :] = sums[1:2, :]
    for k in range(members):
        at = slice(k * size, (k + 1) * size)
        recv, here = recv_one, k
        if k >= members // 2:
            recv, here = recv_two, k - members // 2
        got = recv[here * size : (here + 1) * size, :]
        out[k, 0:size, :] = (keep[at, :].astype(F32) + got.astype(F32)).astype(BF16)
        if k < members // 2:
            rows, span = c2_place(k)
            out[k, size:, :] = c2[rows, span].astype(BF16)
        else:
            out[k, size:, :] = two_parts(lines[table_place(k), :])
        pltpu.make_async_copy(out.at[k], out_far.at[k], sems.at[k]).start()
    for k in range(members):
        pltpu.make_async_copy(out.at[k], out_far.at[k], sems.at[k]).wait()


def c2_place(k):
    return slice(k % 2 * SHORT, (k % 2 + 1) * SHORT), slice(k // 2 * LANES, (k // 2 + 1) * LANES)


def table_place(k):
    at = (k - CUBE // 2) * SHORT // 2
    return slice(at, at + SHORT // 2)


def riders(batch, parts):
    plain = sum(p.astype(F32) for p in parts).astype(BF16)
    fine = two_parts(sum(one_part(p) for p in parts))
    return jnp.where(batch[0] % CUBE < CUBE // 2, plain.astype(F32), fine.astype(F32)).astype(BF16)


def cube_kernel(batch, got, c1, out):
    members = got.shape[0]
    size = got.shape[1] - SHORT
    out[0:size, :] = sum(got[k, 0:size, :].astype(F32) for k in range(members)).astype(BF16)
    out[size : size + SHORT, :] = riders(batch, [got[k, size:, :] for k in range(members)])
    out[size + SHORT :, :] = c1[...]


def add_kernel(batch, a, b, after, out):
    size = a.shape[0] - SHORT - 32
    for span in (slice(0, size), slice(size + SHORT, a.shape[0])):
        out[span, :] = (a[span, :].astype(F32) + b[span, :].astype(F32)).astype(BF16)
    ride = slice(size, size + SHORT)
    out[ride, :] = riders(batch, [a[ride, :], b[ride, :]])


def relay_kernel(batch, *refs):
    parts, (one, two, out) = refs[:CUBE], refs[-3:]
    me = batch[0] % CUBE
    for k, part in enumerate(parts):
        out[me ^ k] = part[...]
    one[...] = out[: CUBE // 2]
    two[...] = out[CUBE // 2 :]


def piece_of(got, k):
    count = got[0].shape[0]
    return got[k // count].at[k % count]


def unpack_half(which, got, lw, bw, vw, stage, stage_b, sems):
    members = 2 * got[0].shape[0]
    size = stage.shape[0] // members
    linear_rows, width = lw.shape
    options = bw.shape[0]
    half = (linear_rows + options * width + width) // 2
    rest = linear_rows - half
    group = options // 3

    def first_copies():
        spans = [(k * size, min((k + 1) * size, half)) for k in range(members)]
        return [
            pltpu.make_async_copy(stage.at[a:b], lw.at[a:b], sems.at[k])
            for k, (a, b) in enumerate(spans)
        ]

    def second_copies():
        copies = [pltpu.make_async_copy(stage.at[0:rest], lw.at[half:], sems.at[0])]
        for k in range(options // group):
            part = slice(k * group, (k + 1) * group)
            copies.append(pltpu.make_async_copy(stage_b.at[part], bw.at[part], sems.at[1 + k]))
        last = stage.at[rest : rest + width]
        copies.append(pltpu.make_async_copy(last, vw, sems.at[len(copies)]))
        return copies

    @pl.when(which == 0)
    def _():
        for k, copy in enumerate(first_copies()):
            start, end = k * size, min((k + 1) * size, half)
            stage[start:end, :] = piece_of(got, k)[0 : end - start, :].astype(F32)
            copy.start()

    @pl.when(which == 1)
    def _():
        def rows(start, end):
            parts = []
            while start < end:
                k, at = start // size, start % size
                count = min(size - at, end - start)
                parts.append(piece_of(got, k)[at : at + count, :])
                start += count
            value = parts[0] if len(parts) == 1 else jnp.concatenate(parts, axis=0)
            return value.astype(F32)

        copies = second_copies()
        stage[0:rest, :] = rows(0, rest)
        copies[0].start()
        for o in range(options):
            stage_b[o] = rows(rest + o * width, rest + (o + 1) * width)
            if o % group == group - 1:
                copies[1 + o // group].start()
        at = rest + options * width
        stage[rest : rest + width, :] = rows(at, at + width)
        copies[-1].start()

    def finish():
        for half_at, copies in ((0, first_copies), (1, second_copies)):

            @pl.when(which == half_at)
            def _():
                for copy in copies():
                    copy.wait()

    return finish


def own_kernel(section, one, two, lw, bw, vw, stage, stage_b, sems):
    unpack_half(section[0], (one, two), lw, bw, vw, stage, stage_b, sems)()


def unpack_kernel(section, *refs):
    mine, other, refs = refs[0:2], refs[2:4], refs[4:]
    lw, bw, vw = refs[3:6]
    little = (len(refs) - 10) // 2
    far, near = refs[6 : 6 + little], refs[6 + little : 6 + 2 * little]
    loss, c1, b1, c2, b2, lb, bb, hw, hb, vb, ow, ob = near
    stage, stage_b, lines, sems = refs[-4:]
    options = bw.shape[0]
    k1, k2 = c1.shape[0], c2.shape[0]
    size = stage.shape[0] // CUBE
    finish = unpack_half(1 - section[0], other, lw, bw, vw, stage, stage_b, sems)
    grad = [jnp.zeros((k1, LANES), F32) for _ in range(2)]
    ride = slice(size, size + SHORT)
    for k in range(CUBE):
        views = piece_of(mine, k), piece_of(other, k)
        if k < CUBE // 2:
            c2[c2_place(k)] = sum(v[ride, :].astype(F32) for v in views)
        else:
            lines[table_place(k), :] = sum(one_part(v[ride, :]) for v in views)
        for view in views:
            for h in range(2):
                at = size + SHORT + h * k1
                grad[h] += view[at : at + k1, :].astype(F32)
    for part in range(2):
        c1[:, part * LANES : (part + 1) * LANES] = grad[part]
    bb[...] = lines[0:options, :]
    vb[...] = lines[AT_VB, :]
    ow[...] = lines[AT_OW, :]
    hw[...] = lines[AT_HW, :]
    lb[...] = lines[AT_LB, :]
    scalars = lines[AT_SCALARS, :]
    loss[...] = scalars[:, 0:1]
    hb[...] = scalars[:, 1:3]
    ob[...] = scalars[:, 3:4]
    b1[...] = lines[AT_B1, 0:k1]
    b2[...] = lines[AT_B2, 0:k2]
    copies = [
        pltpu.make_async_copy(a, b, sems.at[CUBE + k]) for k, (a, b) in enumerate(zip(near, far))
    ]
    for copy in copies:
        copy.start()
    finish()
    for copy in copies:
        copy.wait()


def numbers_kernel(
    options,
    depth,
    targets,
    destination,
    b1,
    b2,
    lb,
    bb,
    hw,
    vb,
    ow,
    hb,
    ob,
    out,
    table,
):
    levels, kinds = options.shape[0], targets.shape[0]
    slots = depth.shape[1]
    rows = [options[...].astype(F32), depth[...].astype(F32)]
    rows += [targets[k] for k in range(kinds)]
    rows.append(jnp.zeros((LANES - levels - 1 - kinds * levels, slots), F32))
    out[...] = jnp.transpose(jnp.concatenate(rows, axis=0))
    table[...] = jnp.zeros_like(table)
    table[0 : bb.shape[0], :] = bb[...]
    table[AT_VB, :] = vb[...]
    table[AT_OW, :] = ow[...].astype(F32)
    table[AT_HW, :] = hw[...].astype(F32)
    table[AT_LB, :] = lb[...]
    table[AT_B1, 0 : b1.shape[1]] = b1[...]
    table[AT_B2, 0 : b2.shape[1]] = b2[...]
    lane = iota((1, LANES), 1)
    scalars = jnp.zeros((1, LANES), F32)
    for k, value in ((1, hb[:, 0:1]), (2, hb[:, 1:2]), (3, ob[...])):
        scalars = jnp.where(lane == k, value, scalars)
    table[AT_SCALARS, :] = scalars
    for k in range(slots // LANES):
        part = destination[:, k * LANES : (k + 1) * LANES]
        table[AT_DEST + k : AT_DEST + k + 1, :] = part.astype(F32)


def whole(shape):
    zeros = (0,) * len(shape)
    return pl.BlockSpec(shape, lambda *_: zeros)


ANYWHERE = pl.BlockSpec(memory_space=pl.ANY)
SCALARS = pl.BlockSpec(memory_space=pltpu.SMEM)


def params():
    return pltpu.CompilerParams(vmem_limit_bytes=VMEM_BYTES)


def shape_of(*shape, dtype=F32):
    return jax.ShapeDtypeStruct(shape, dtype)


def cost(microseconds):
    return pl.CostEstimate(
        flops=int(1.1e9 * microseconds), bytes_accessed=int(3.6e6 * microseconds), transcendentals=0
    )


def stays(value):
    return pltpu.with_memory_space_constraint(value, pltpu.HBM)


def held_near(value):
    return pltpu.with_memory_space_constraint(value, pltpu.VMEM)


def encode(section, frames, w1t, w2t, lw, table):
    img = frames.shape[0]
    blocks = img // 4
    side = blocks - 1
    k1, k2, width = w1t.shape[0], w2t.shape[0], lw.shape[1]
    flat = lw.shape[0]
    vmem = pltpu.VMEM
    near = pl.BlockSpec(memory_space=vmem)
    grid_one = (blocks, side, k1, LANES)
    return pl.pallas_call(
        encode_kernel,
        in_specs=[SCALARS, ANYWHERE, near, near, ANYWHERE, near],
        out_specs=[ANYWHERE] * 3 + [near] * 3,
        out_shape=(
            pltpu.HBM(grid_one, BF16),
            pltpu.HBM(grid_one, BF16),
            pltpu.HBM((flat, LANES), BF16),
            shape_of(flat, LANES, dtype=BF16),
            shape_of(width, LANES, dtype=BF16),
            shape_of(width, LANES),
        ),
        scratch_shapes=[
            vmem((img, img, frames.shape[2], LANES), BF16),
            vmem(lw.shape, BF16),
            vmem(grid_one, BF16),
            vmem(grid_one, BF16),
            vmem((flat, LANES), BF16),
            vmem((2 * REACH * k1, 256), BF16),
            vmem((2 * k1, 64), BF16),
            vmem((6 * k2, LANES), BF16),
            vmem((k1, LANES), F32),
            vmem((k2, LANES), F32),
            vmem((side, k1, LANES), F32),
            vmem((side // 2 - 1, k2, LANES), F32),
            pltpu.SemaphoreType.DMA((4, max(blocks // STEP, 3))),
        ],
        compiler_params=params(),
        cost_estimate=cost(9),
        name="encode",
    )(section, frames, w1t, w2t, lw, table)


def plan(section, slots, enc, s3, h2, branch_w, value_w, table, per_pair, depth, half_rows):
    width = enc.shape[0]
    options = branch_w.shape[0]
    two = 2 * width
    pairs = options // 2
    outs = (
        shape_of(half_rows, LANES, dtype=BF16),
        shape_of(half_rows // 2, LANES, dtype=BF16),
        shape_of(half_rows // 2, LANES, dtype=BF16),
        shape_of(TABLE, LANES),
        shape_of(width, LANES, dtype=BF16),
    )
    vmem = pltpu.VMEM
    near = pl.BlockSpec(memory_space=vmem)
    return pl.pallas_call(
        functools.partial(plan_kernel, per_pair=per_pair, depth=depth),
        in_specs=[SCALARS, near, near, near, near, ANYWHERE, near, near],
        out_shape=outs,
        scratch_shapes=[
            vmem((2, half_rows, LANES), BF16),
            vmem((options * width, width + 16), BF16),
            vmem((width + 16, width + 16), BF16),
            vmem((width, width + 16), BF16),
            vmem((width, LANES), F32),
            vmem((16, LANES), F32),
            vmem((options * width, LANES), F32),
            vmem((depth, options * width, LANES), F32),
            vmem((depth, pairs, width, two), F32),
            vmem((depth, pairs, width + 16, two), BF16),
            vmem((depth, pairs, width, two), BF16),
            vmem((depth, options * width, LANES), BF16),
            vmem(branch_w.shape, BF16),
            pltpu.SemaphoreType.DMA,
        ],
        compiler_params=params(),
        cost_estimate=cost(11),
        name="plan",
    )(section, slots, enc, s3, h2, branch_w, value_w, table)


def back(g3, lw, s2, s1, h1, w2t):
    _, side, k1 = s1.shape[:3]
    k2 = w2t.shape[0]
    inner = side // 2 - 1
    padded = (side + 2, side, k1, LANES)
    near = pl.BlockSpec(memory_space=pltpu.VMEM)
    return pl.pallas_call(
        back_kernel,
        in_specs=[near] * 6,
        out_shape=(shape_of(*padded, dtype=BF16), shape_of(k2, 256), shape_of(8, LANES)),
        scratch_shapes=[
            pltpu.VMEM((LANES, 6 * k2), BF16),
            pltpu.VMEM((inner + 2, inner, k2, LANES), BF16),
        ],
        compiler_params=params(),
        cost_estimate=cost(25),
        name="back",
    )(g3, lw, s2, s1, h1, w2t)


def first(section, frames, g1, w1t, other, after, channels, draw):
    img, _, stack, _ = frames.shape
    k1 = g1.shape[2]
    band = (STEP * 4 * COLS * channels, (STEP + 1) * NEAR * k1)
    near = pl.BlockSpec(memory_space=pltpu.VMEM)
    return pl.pallas_call(
        functools.partial(first_kernel, draw=draw),
        in_specs=[SCALARS, ANYWHERE, near, near, ANYWHERE, ANYWHERE],
        out_specs=[near, ANYWHERE, near],
        out_shape=[
            shape_of(2 * k1, LANES, dtype=BF16),
            shape_of(img, img, channels, 2 * LANES),
            shape_of(*band, dtype=BF16),
        ],
        scratch_shapes=[
            pltpu.VMEM((img, img, stack, LANES), BF16),
            pltpu.VMEM((STEP * 4 * COLS * stack, (STEP + 1) * NEAR * k1), F32),
            pltpu.VMEM((STEP * draw + 1,) + g1.shape[1:], BF16),
            pltpu.VMEM((2, 2, 4 * STEP, img, channels, LANES), F32),
            pltpu.SemaphoreType.DMA((img // 4 // STEP + 1,)),
            pltpu.SemaphoreType.DMA((2, 2)),
        ],
        compiler_params=params(),
        cost_estimate=cost(45),
        name="first",
    )(section, frames, g1, w1t, other, after)


def pixels(section, band, mine, other, after, done, start, steps):
    img, _, channels, _ = done.shape
    near = pl.BlockSpec(memory_space=pltpu.VMEM)
    return pl.pallas_call(
        functools.partial(pixels_kernel, start=start),
        in_specs=[SCALARS, near, near, ANYWHERE, ANYWHERE, ANYWHERE],
        out_specs=[ANYWHERE, near],
        out_shape=[shape_of(*done.shape), shape_of(8, LANES)],
        scratch_shapes=[
            pltpu.VMEM((2, 2, 4 * STEP, img, channels, LANES), F32),
            pltpu.VMEM((STEP * steps + 1,) + mine.shape[1:], BF16),
            pltpu.SemaphoreType.DMA((3, 2)),
        ],
        input_output_aliases={5: 0},
        compiler_params=params(),
        cost_estimate=cost(1 + 0.9 * steps),
        name="pixels",
    )(section, band, mine, other, after, done)


def small_call(
    kernel, outs, operands, scratch=(), name=None, place=None, after=(), weight=0.3, far=False
):
    specs = [pl.BlockSpec(memory_space=pltpu.VMEM)] * len(operands)
    if place is not None:
        operands = (*place, *operands)
        specs = [pl.BlockSpec(memory_space=pltpu.SMEM)] * len(place) + specs
    return pl.pallas_call(
        kernel,
        in_specs=specs + [ANYWHERE] * len(after),
        out_specs=jax.tree.map(
            lambda _: ANYWHERE if far else pl.BlockSpec(memory_space=pltpu.VMEM), outs
        ),
        out_shape=outs,
        scratch_shapes=list(scratch),
        compiler_params=params(),
        cost_estimate=cost(weight),
        name=name,
    )(*operands, *after)


def round_up(value, step):
    return -(-value // step) * step


def swapped(value):
    return lax.ppermute(value, "section", [(0, 1), (1, 0)])


def exchanged(value, groups=None):
    return lax.all_to_all(
        value, "batch", split_axis=0, concat_axis=0, axis_index_groups=groups, tiled=True
    )


def partner(value, distance):
    count = lax.axis_size("batch")
    return lax.ppermute(value, "batch", [(b, b ^ distance) for b in range(count)])


def local(
    frames,
    destination,
    options,
    depth,
    targets,
    conv_one,
    bias_one,
    conv_two,
    bias_two,
    linear_w,
    linear_b,
    branch_w,
    branch_b,
    head_w,
    head_b,
    value_w,
    value_b,
    out_w,
    out_b,
):
    section = lax.axis_index("section").astype(jnp.int32)[None]
    peers = lax.axis_size("batch")
    frame_count = frames.shape[3]
    per_pair = frame_count // peers
    levels = options.shape[0]
    frames = stays(frames.transpose(1, 2, 0, 3))
    w1t, w2t = stays(conv_one.T), stays(conv_two.T)
    branch_w, value_w = stays(branch_w), stays(value_w)
    encoder_params = (w1t, bias_one, w2t, bias_two, linear_w, linear_b)
    planner_params = (branch_w, branch_b, head_w.T, head_b, value_w, value_b, out_w.T, out_b)
    width = linear_w.shape[1]
    big_rows = linear_w.shape[0] + (branch_w.shape[0] + 1) * width
    size = round_up(-(-big_rows // (2 * CUBE)), 16)

    tiny = (bias_one, bias_two, linear_b, branch_b, head_w.T, value_b, out_w.T)
    tiny = [stays(v if v.ndim > 1 else v[None, :]) for v in tiny]
    numbers, table = pl.pallas_call(
        numbers_kernel,
        in_specs=[pl.BlockSpec(memory_space=pltpu.VMEM)] * (6 + len(tiny)),
        out_shape=[shape_of(frame_count, LANES), shape_of(TABLE, LANES)],
        compiler_params=params(),
        cost_estimate=cost(1),
        name="numbers",
    )(
        stays(options),
        stays(depth[None, :]),
        stays(targets),
        stays(destination[None, :]),
        *tiny,
        stays(head_b[None, :]),
        out_b[None, :],
    )
    slots = exchanged(numbers.reshape(peers, per_pair, LANES)).reshape(frame_count, LANES)

    h1, s1, s2, h2, enc, s3 = encode(section, frames, w1t, w2t, stays(linear_w), table)
    keep, send_one, send_two, small, g3 = plan(
        section, slots, enc, s3, h2, branch_w, value_w, table, per_pair, levels, CUBE * size
    )
    recv = swapped(send_one), swapped(send_two)
    channels = frames.shape[2] // lax.axis_size("section")
    g1, c2, sums = back(g3, linear_w, s2, s1, h1, w2t)
    other = swapped(g1)
    g1 = held_near(g1)
    place = (lax.axis_index("batch").astype(jnp.int32)[None],)
    cubes = [list(range(c, c + CUBE)) for c in range(0, peers, CUBE)]
    bf16 = functools.partial(shape_of, dtype=BF16)
    pieces = small_call(
        merge_kernel,
        bf16(CUBE, size + SHORT, LANES),
        (keep, *recv, small, c2, sums),
        [
            pltpu.VMEM((TABLE, LANES), F32),
            pltpu.VMEM((CUBE, size + SHORT, LANES), BF16),
            pltpu.SemaphoreType.DMA((CUBE,)),
        ],
        name="merge",
        far=True,
        weight=30,
    )
    got = exchanged(pieces, cubes)
    c1, frames_grad, band = first(section, frames, g1, w1t, other, pieces, channels, DRAW)
    piece = bf16(size + SHORT + c1.shape[0], LANES)
    keep = small_call(cube_kernel, piece, (got, c1), name="cube", place=place)
    distance = CUBE
    while distance < peers:
        recv = partner(keep, distance)
        if distance == CUBE:
            left = frames.shape[0] // 4 // STEP - DRAW
            frames_grad, token = pixels(
                section, band, g1, other, keep, frames_grad, DRAW, left
            )
        distance *= 2
        keep = small_call(
            add_kernel, piece, (keep, recv), name="add", place=place, after=(token,)
        )
    parts = [keep] + [partner(keep, k) for k in range(1, CUBE)]
    got = small_call(
        relay_kernel,
        [bf16(CUBE // 2, *piece.shape)] * 2,
        parts,
        [pltpu.VMEM((CUBE, *piece.shape), BF16)],
        name="relay",
        place=place,
    )
    got_other = [swapped(v) for v in got]
    shapes = [p.shape for p in encoder_params + planner_params]
    near = pl.BlockSpec(memory_space=pltpu.VMEM)
    flat = [shape_of(*(v if len(v) > 1 else (1,) + v)) for v in [(1, 1)] + shapes]
    large = [flat[k] for k in (5, 7, 11)]
    staged = [
        pltpu.VMEM((CUBE * size, LANES), F32),
        pltpu.VMEM(branch_w.shape, F32),
    ]
    little = [v for k, v in enumerate(flat) if k not in (5, 7, 11)]
    sems = pltpu.SemaphoreType.DMA((CUBE + len(little),))
    begun = pl.pallas_call(
        own_kernel,
        in_specs=[SCALARS, near, near],
        out_specs=[ANYWHERE] * 3,
        out_shape=large,
        scratch_shapes=[*staged, sems],
        compiler_params=params(),
        cost_estimate=cost(1),
        name="own",
    )(section, *got)
    ends = pl.pallas_call(
        unpack_kernel,
        in_specs=[SCALARS] + [near] * 4 + [ANYWHERE] * 3,
        out_specs=[ANYWHERE] * (3 + len(little)),
        out_shape=large + little,
        scratch_shapes=[pltpu.VMEM(v.shape, F32) for v in little]
        + [*staged, pltpu.VMEM((TABLE, LANES), F32), sems],
        input_output_aliases={5: 0, 6: 1, 7: 2},
        compiler_params=params(),
        cost_estimate=cost(1.5),
        name="unpack",
    )(section, *got, *got_other, *begun)
    rest = list(ends[3:])
    for k, at in enumerate((5, 7, 11)):
        rest.insert(at, ends[k])
    rest = [v.reshape(s) for v, s in zip(rest, [()] + shapes)]
    for at in (1, 3, 9, 13):
        rest[at] = rest[at].T
    return (rest[0], frames_grad.transpose(2, 0, 1, 3), *rest[1:])


def solution(mesh):
    placed = (
        P(None, None, None, "batch"),
        P("batch"),
        P(None, "batch"),
        P("batch"),
        P(None, None, "batch"),
    ) + (P(),) * 14
    return jax.shard_map(
        local,
        mesh=mesh,
        in_specs=placed,
        out_specs=(P(), P("section", None, None, "batch")) + (P(),) * 14,
        check_vma=False,
    )
```

profile of v0, /device:TPU:0, one launch (start us, length us, event | category | flops | bytes accessed | tf_op | source)
XLA Modules:
  0.0 73.2 jit_solution(6486759419021899450)
XLA Ops:
  1.3 1.6 %numbers.1 = (f32[256,128]{1,0:T(8,128)}, f32[32,128]{1,0:T(8,128)S(1)}) custom-call(s32[3,256]{1,0:T(4,128)} %options.1, s32[1,256]{1,0:T(1,128)} %bitcast.38, f32[3,3,256]{2,1,0:T(4,128)} %targets.1, s32[1,256]{1,0:T(1,128)} %bitcast.39, f32[1,16]{1,0:T(1,128)} %bitcast.40, f32[1,32]{1,0:T(1,128)} %bitcast.41, f32[1,128]{1,0:T(1,128)} %bitcast.42, ...), custom_call_target="tpu_custom_call" | custom-call | flops 1100000000 | bytes 3600000 | tf_op jit(solution)/shard_map/numbers/pallas_call | solution.py:1358
  2.9 8.3 %all-to-all-start = ((f32[16,16,128]{2,1,0:T(8,128)}), f32[16,16,128]{2,1,0:T(8,128)S(1)}, u32[]{:S(2)}, u32[]{:S(2)}) async-start(f32[16,16,128]{2,1,0:T(8,128)} %bitcast.12), calls=%async_computation | async-start | bytes 262144 | tf_op jit(solution)/shard_map/all_to_all | solution.py:1311
  11.2 7.7 %encode.1 = (bf16[21,20,16,128]{3,2,1,0:T(8,128)(2,1)}, bf16[21,20,16,128]{3,2,1,0:T(8,128)(2,1)}, bf16[2592,128]{1,0:T(8,128)(2,1)}, bf16[2592,128]{1,0:T(8,128...) custom-call(s32[1]{0:T(128)} %bitcast.section, bf16[84,84,4,256]{3,2,1,0:T(4,128)(2,1)} %bitcast.32, ...), custom_call_target="tpu_custom_call" | custom-call | flops 9900000256 | bytes 32400000 | tf_op jit(solution)/shard_map/encode/pallas_call | solution.py:1140
  19.0 8.5 %plan.1 = (bf16[2560,128]{1,0:T(8,128)(2,1)S(1)}, bf16[1280,128]{1,0:T(8,128)(2,1)S(1)}, bf16[1280,128]{1,0:T(8,128)(2,1)S(1)}, f32[32,128]{1,0:T(8,128)S(1)}, bf16[128,128]{1,0:T(8,128)(2,1)S(1)}) custom-call(s32[1]{0:T(128)} %bitcast.section, f32[256,128]{1,0:T(8,128)S(1)} %bitcast.30, bf16[128,128]{1,0:T(8,128)(2,1)S(1)} %get-tuple-element.59.enc, ...), custom_call_target="tpu_custom_call" | custom-call | flops 12099999744 | bytes 39600000 | tf_op jit(solution)/shard_map/plan/pallas_call | solution.py:1187
  28.1 2.7 %back.1 = (bf16[22,20,16,128]{3,2,1,0:T(8,128)(2,1)S(1)}, f32[32,256]{1,0:T(8,128)S(1)}, f32[8,128]{1,0:T(8,128)S(1)}) custom-call(bf16[128,128]{1,0:T(8,128)(2,1)S(1)} %get-tuple-element.66.g3, bf16[2592,128]{1,0:T(8,128)(2,1)S(1)} %copy-done, bf16[2592,128]{1,0:T(8,128)(2,1)S(1)} %copy-done.3, bf16[21,20,16,128]{3,2,1,0:T(8,128)(2,1)S(1)} %copy-done.2, ...), custom_call_target="tpu_custom_call" | custom-call | flops 27499999232 | bytes 90000000 | tf_op jit(solution)/shard_map/back/pallas_call | solution.py:1219
  30.9 0.9 %merge.1.after = bf16[8,336,128]{2,1,0:T(8,128)(2,1)} custom-call(bf16[2560,128]{1,0:T(8,128)(2,1)S(1)} %get-tuple-element.62.keep, bf16[1280,128]{1,0:T(8,128)(2,1)S(1)} %collective-permute-done.recv_one, bf16[1280,128]{1,0:T(8,128)(2,1)S(1)} %collective-permute-done.1.recv_two, f32[32,128]{1,0:T(8,128)S(1)} %get-tuple-element.65.small, ...), custom_call_target="tpu_custom_call" | custom-call | flops 32999999488 | bytes 108000000 | tf_op jit(solution)/shard_map/merge/pallas_call | solution.py:1288
  31.8 5.0 %all-to-all-start.1 = ((bf16[8,336,128]{2,1,0:T(8,128)(2,1)}), bf16[8,336,128]{2,1,0:T(8,128)(2,1)S(1)}, u32[]{:S(2)}, u32[]{:S(2)}) async-start(bf16[8,336,128]{2,1,0:T(8,128)(2,1)} %merge.1.after), calls=%async_computation.1 | async-start | bytes 1376256 | tf_op jit(solution)/shard_map/all_to_all | solution.py:1311
  36.8 10.1 %first.1 = (bf16[32,128]{1,0:T(8,128)(2,1)S(1)}, f32[84,84,2,256]{3,2,1,0:T(2,128)}, bf16[288,256]{1,0:T(8,128)(2,1)S(1)}) custom-call(s32[1]{0:T(128)} %bitcast.section, bf16[84,84,4,256]{3,2,1,0:T(4,128)(2,1)} %bitcast.33, bf16[22,20,16,128]{3,2,1,0:T(8,128)(2,1)S(1)} %get-tuple-element.72.g1.mine, bf16[16,256]{1,0:T(8,128)(2,1)} %bitcast.37, ...), custom_call_target="tpu_custom_call" | custom-call | flops 49500000256 | bytes 162000000 | tf_op jit(solution)/shard_map/first/pallas_call | solution.py:1238
  46.9 1.2 %all-to-all-done.1.got = bf16[8,336,128]{2,1,0:T(8,128)(2,1)S(1)} async-done(((bf16[8,336,128]{2,1,0:T(8,128)(2,1)}), bf16[8,336,128]{2,1,0:T(8,128)(2,1)S(1)}, u32[]{:S(2)}, u32[]{:S(2)}) %all-to-all-start.1) | async-done | bytes 688160 | tf_op jit(solution)/shard_map/all_to_all | solution.py:1311
  48.1 2.4 %collective-permute-start.3 = (bf16[368,128]{1,0:T(8,128)(2,1)S(1)}, bf16[368,128]{1,0:T(8,128)(2,1)S(1)}, u32[]{:S(2)}, u32[]{:S(2)}) collective-permute-start(bf16[368,128]{1,0:T(8,128)(2,1)S(1)} %cube.1.after.a), channel_id=1, source_target_pairs={{0,8},{1,9},{2,10},{3,11},{4,12},{5,13},{6,14},{7,15},{8,0},{9,1},... | collective-permute-start | bytes 282632 | tf_op jit(solution)/shard_map/ppermute | solution.py:1318
  50.6 4.7 %pixels.1 = (f32[84,84,2,256]{3,2,1,0:T(2,128)}, f32[8,128]{1,0:T(8,128)S(1)}) custom-call(s32[1]{0:T(128)} %bitcast.section, bf16[288,256]{1,0:T(8,128)(2,1)S(1)} %get-tuple-element.74.band, bf16[22,20,16,128]{3,2,1,0:T(8,128)(2,1)S(1)} %get-tuple-element.72.g1.mine, ...), custom_call_target="tpu_custom_call", output_to_operand_aliasing={{0}: (5, {})} | custom-call | flops 4070000128 | bytes 13320000 | tf_op jit(solution)/shard_map/pixels/pallas_call | solution.py:1264
  55.7 2.4 %collective-permute-start.10 = (bf16[368,128]{1,0:T(8,128)(2,1)S(1)}, bf16[368,128]{1,0:T(8,128)(2,1)S(1)}, u32[]{:S(2)}, u32[]{:S(2)}) collective-permute-start(bf16[368,128]{1,0:T(8,128)(2,1)S(1)} %add.1.refs_0_), channel_id=1, source_target_pairs={{0,7},{1,6},{2,5},{3,4},{4,3},{5,2},{6,1},{7,0},{8,15},{9,14},{10,... | collective-permute-start | bytes 282632 | tf_op jit(solution)/shard_map/ppermute | solution.py:1318
  58.1 0.9 %collective-permute-start.9 = (bf16[368,128]{1,0:T(8,128)(2,1)S(1)}, bf16[368,128]{1,0:T(8,128)(2,1)S(1)}, u32[]{:S(2)}, u32[]{:S(2)}) collective-permute-start(bf16[368,128]{1,0:T(8,128)(2,1)S(1)} %add.1.refs_0_), channel_id=1, source_target_pairs={{0,6},{1,7},{2,4},{3,5},{4,2},{5,3},{6,0},{7,1},{8,14},{9,15},{10,... | collective-permute-start | bytes 282632 | tf_op jit(solution)/shard_map/ppermute | solution.py:1318
  58.9 1.7 %collective-permute-start.8 = (bf16[368,128]{1,0:T(8,128)(2,1)S(1)}, bf16[368,128]{1,0:T(8,128)(2,1)S(1)}, u32[]{:S(2)}, u32[]{:S(2)}) collective-permute-start(bf16[368,128]{1,0:T(8,128)(2,1)S(1)} %add.1.refs_0_), channel_id=1, source_target_pairs={{0,5},{1,4},{2,7},{3,6},{4,1},{5,0},{6,3},{7,2},{8,13},{9,12},{10,... | collective-permute-start | bytes 282632 | tf_op jit(solution)/shard_map/ppermute | solution.py:1318
  60.7 0.9 %collective-permute-start.7 = (bf16[368,128]{1,0:T(8,128)(2,1)S(1)}, bf16[368,128]{1,0:T(8,128)(2,1)S(1)}, u32[]{:S(2)}, u32[]{:S(2)}) collective-permute-start(bf16[368,128]{1,0:T(8,128)(2,1)S(1)} %add.1.refs_0_), channel_id=1, source_target_pairs={{0,4},{1,5},{2,6},{3,7},{4,0},{5,1},{6,2},{7,3},{8,12},{9,13},{10,... | collective-permute-start | bytes 282632 | tf_op jit(solution)/shard_map/ppermute | solution.py:1318
  61.6 1.8 %collective-permute-start.6 = (bf16[368,128]{1,0:T(8,128)(2,1)S(1)}, bf16[368,128]{1,0:T(8,128)(2,1)S(1)}, u32[]{:S(2)}, u32[]{:S(2)}) collective-permute-start(bf16[368,128]{1,0:T(8,128)(2,1)S(1)} %add.1.refs_0_), channel_id=1, source_target_pairs={{0,3},{1,2},{2,1},{3,0},{4,7},{5,6},{6,5},{7,4},{8,11},{9,10},{10,... | collective-permute-start | bytes 282632 | tf_op jit(solution)/shard_map/ppermute | solution.py:1318
  63.3 0.6 collective-permute-start.5
  63.9 0.9 %collective-permute-done.9.refs_6_ = bf16[368,128]{1,0:T(8,128)(2,1)S(1)} collective-permute-done((bf16[368,128]{1,0:T(8,128)(2,1)S(1)}, bf16[368,128]{1,0:T(8,128)(2,1)S(1)}, u32[]{:S(2)}, u32[]{:S(2)}) %collective-permute-start.9) | collective-permute-done | bytes 94240 | tf_op jit(solution)/shard_map/ppermute | solution.py:1318
  64.8 1.0 %collective-permute-start.4 = (bf16[368,128]{1,0:T(8,128)(2,1)S(1)}, bf16[368,128]{1,0:T(8,128)(2,1)S(1)}, u32[]{:S(2)}, u32[]{:S(2)}) collective-permute-start(bf16[368,128]{1,0:T(8,128)(2,1)S(1)} %add.1.refs_0_), channel_id=1, source_target_pairs={{0,1},{1,0},{2,3},{3,2},{4,5},{5,4},{6,7},{7,6},{8,9},{9,8},{10,11... | collective-permute-start | bytes 282632 | tf_op jit(solution)/shard_map/ppermute | solution.py:1318
  66.3 0.7 %collective-permute-done.7.refs_4_ = bf16[368,128]{1,0:T(8,128)(2,1)S(1)} collective-permute-done((bf16[368,128]{1,0:T(8,128)(2,1)S(1)}, bf16[368,128]{1,0:T(8,128)(2,1)S(1)}, u32[]{:S(2)}, u32[]{:S(2)}) %collective-permute-start.7) | collective-permute-done | bytes 94240 | tf_op jit(solution)/shard_map/ppermute | solution.py:1318
  67.1 1.2 %collective-permute-done.6.refs_3_ = bf16[368,128]{1,0:T(8,128)(2,1)S(1)} collective-permute-done((bf16[368,128]{1,0:T(8,128)(2,1)S(1)}, bf16[368,128]{1,0:T(8,128)(2,1)S(1)}, u32[]{:S(2)}, u32[]{:S(2)}) %collective-permute-start.6) | collective-permute-done | bytes 94240 | tf_op jit(solution)/shard_map/ppermute | solution.py:1318
  68.7 0.7 collective-permute-done.4.refs_1_
  70.1 1.2 %own.1 = (f32[2592,128]{1,0:T(8,128)}, f32[18,128,128]{2,1,0:T(8,128)}, f32[128,128]{1,0:T(8,128)}) custom-call(s32[1]{0:T(128)} %bitcast.section, bf16[4,368,128]{2,1,0:T(8,128)(2,1)S(1)} %get-tuple-element.77.one.refs_0_, bf16[4,368,128]{2,1,0:T(8,128)(2,1)S(1)} %get-tuple-element.78.two.refs_1_), custom_call_target="tpu_custom_call" | custom-call | flops 1100000000 | bytes 3600000 | tf_op jit(solution)/shard_map/own/pallas_call | solution.py:1437
  71.8 1.3 %unpack.1 = (f32[2592,128]{1,0:T(8,128)}, f32[18,128,128]{2,1,0:T(8,128)}, f32[128,128]{1,0:T(8,128)}, f32[1,1]{1,0:T(1,128)}, f32[16,256]{1,0:T(8,128)}, /*inde...) custom-call(s32[1]{0:T(128)} %bitcast.section, ...), custom_call_target="tpu_custom_call", output_to_operand_aliasing={{0}: (5, {}), {1}: (6, {}), {2}: (7, {})} | custom-call | flops 1650000000 | bytes 5400000 | tf_op jit(solution)/shard_map/unpack/pallas_call | solution.py:1447
  (26 shorter events, 3.4 us)
Async XLA Ops:
  2.9 16.1 %all-to-all-start = ((f32[16,16,128]{2,1,0:T(8,128)}), f32[16,16,128]{2,1,0:T(8,128)S(1)}, u32[]{:S(2)}, u32[]{:S(2)}) async-start(f32[16,16,128]{2,1,0:T(8,128)} %bitcast.12), calls=%async_computation | async-start | bytes 262144 | tf_op jit(solution)/shard_map/all_to_all | solution.py:1311
  19.0 9.1 %copy-start = (bf16[2592,128]{1,0:T(8,128)(2,1)S(1)}, bf16[2592,128]{1,0:T(8,128)(2,1)}, u32[]{:S(2)}) copy-start(bf16[2592,128]{1,0:T(8,128)(2,1)} %lw.1) | copy-start | bytes 1990660
  19.0 9.1 %copy-start.1 = (bf16[21,20,16,128]{3,2,1,0:T(8,128)(2,1)S(1)}, bf16[21,20,16,128]{3,2,1,0:T(8,128)(2,1)}, u32[]{:S(2)}) copy-start(bf16[21,20,16,128]{3,2,1,0:T(8,128)(2,1)} %get-tuple-element.69.h1) | copy-start | bytes 5160964
  19.0 9.1 %copy-start.2 = (bf16[21,20,16,128]{3,2,1,0:T(8,128)(2,1)S(1)}, bf16[21,20,16,128]{3,2,1,0:T(8,128)(2,1)}, u32[]{:S(2)}) copy-start(bf16[21,20,16,128]{3,2,1,0:T(8,128)(2,1)} %get-tuple-element.68.s1) | copy-start | bytes 5160964
  19.0 9.1 %copy-start.3 = (bf16[2592,128]{1,0:T(8,128)(2,1)S(1)}, bf16[2592,128]{1,0:T(8,128)(2,1)}, u32[]{:S(2)}) copy-start(bf16[2592,128]{1,0:T(8,128)(2,1)} %get-tuple-element.67.s2) | copy-start | bytes 1990660
  27.5 3.4 %collective-permute-start = (bf16[1280,128]{1,0:T(8,128)(2,1)S(1)}, bf16[1280,128]{1,0:T(8,128)(2,1)S(1)}, u32[]{:S(2)}, u32[]{:S(2)}) collective-permute-start(bf16[1280,128]{1,0:T(8,128)(2,1)S(1)} %get-tuple-element.63), channel_id=1, source_target_pairs={{0,16},{16,0},{1,17},{17,1},{2,18},{18,2},{3,19},{19,3},{4,20},{20... | collective-permute-start | bytes 983048 | tf_op jit(solution)/shard_map/ppermute | solution.py:1307
  27.6 3.3 %collective-permute-start.1 = (bf16[1280,128]{1,0:T(8,128)(2,1)S(1)}, bf16[1280,128]{1,0:T(8,128)(2,1)S(1)}, u32[]{:S(2)}, u32[]{:S(2)}) collective-permute-start(bf16[1280,128]{1,0:T(8,128)(2,1)S(1)} %get-tuple-element.64), channel_id=1, source_target_pairs={{0,16},{16,0},{1,17},{17,1},{2,18},{18,2},{3,19},{19,3},{4,20},{20... | collective-permute-start | bytes 983048 | tf_op jit(solution)/shard_map/ppermute | solution.py:1307
  30.7 6.0 %collective-permute-start.2 = (bf16[22,20,16,128]{3,2,1,0:T(8,128)(2,1)S(1)}, bf16[22,20,16,128]{3,2,1,0:T(8,128)(2,1)}, u32[]{:S(2)}, u32[]{:S(2)}) collective-permute-start(bf16[22,20,16,128]{3,2,1,0:T(8,128)(2,1)S(1)} %get-tuple-element.72.g1.mine), channel_id=1, source_target_pairs={{0,16},{16,0},{1,17},{17,1},{2,18},{18,2},{3,19},{19,3},{4,20},{20... | collective-permute-start | bytes 5406728 | tf_op jit(solution)/shard_map/ppermute | solution.py:1307
  31.8 16.2 %all-to-all-start.1 = ((bf16[8,336,128]{2,1,0:T(8,128)(2,1)}), bf16[8,336,128]{2,1,0:T(8,128)(2,1)S(1)}, u32[]{:S(2)}, u32[]{:S(2)}) async-start(bf16[8,336,128]{2,1,0:T(8,128)(2,1)} %merge.1.after), calls=%async_computation.1 | async-start | bytes 1376256 | tf_op jit(solution)/shard_map/all_to_all | solution.py:1311
  48.1 7.5 %collective-permute-start.3 = (bf16[368,128]{1,0:T(8,128)(2,1)S(1)}, bf16[368,128]{1,0:T(8,128)(2,1)S(1)}, u32[]{:S(2)}, u32[]{:S(2)}) collective-permute-start(bf16[368,128]{1,0:T(8,128)(2,1)S(1)} %cube.1.after.a), channel_id=1, source_target_pairs={{0,8},{1,9},{2,10},{3,11},{4,12},{5,13},{6,14},{7,15},{8,0},{9,1},... | collective-permute-start | bytes 282632 | tf_op jit(solution)/shard_map/ppermute | solution.py:1318
  55.7 7.7 %collective-permute-start.10 = (bf16[368,128]{1,0:T(8,128)(2,1)S(1)}, bf16[368,128]{1,0:T(8,128)(2,1)S(1)}, u32[]{:S(2)}, u32[]{:S(2)}) collective-permute-start(bf16[368,128]{1,0:T(8,128)(2,1)S(1)} %add.1.refs_0_), channel_id=1, source_target_pairs={{0,7},{1,6},{2,5},{3,4},{4,3},{5,2},{6,1},{7,0},{8,15},{9,14},{10,... | collective-permute-start | bytes 282632 | tf_op jit(solution)/shard_map/ppermute | solution.py:1318
  58.1 6.8 %collective-permute-start.9 = (bf16[368,128]{1,0:T(8,128)(2,1)S(1)}, bf16[368,128]{1,0:T(8,128)(2,1)S(1)}, u32[]{:S(2)}, u32[]{:S(2)}) collective-permute-start(bf16[368,128]{1,0:T(8,128)(2,1)S(1)} %add.1.refs_0_), channel_id=1, source_target_pairs={{0,6},{1,7},{2,4},{3,5},{4,2},{5,3},{6,0},{7,1},{8,14},{9,15},{10,... | collective-permute-start | bytes 282632 | tf_op jit(solution)/shard_map/ppermute | solution.py:1318
  58.9 7.4 %collective-permute-start.8 = (bf16[368,128]{1,0:T(8,128)(2,1)S(1)}, bf16[368,128]{1,0:T(8,128)(2,1)S(1)}, u32[]{:S(2)}, u32[]{:S(2)}) collective-permute-start(bf16[368,128]{1,0:T(8,128)(2,1)S(1)} %add.1.refs_0_), channel_id=1, source_target_pairs={{0,5},{1,4},{2,7},{3,6},{4,1},{5,0},{6,3},{7,2},{8,13},{9,12},{10,... | collective-permute-start | bytes 282632 | tf_op jit(solution)/shard_map/ppermute | solution.py:1318
  60.7 6.4 %collective-permute-start.7 = (bf16[368,128]{1,0:T(8,128)(2,1)S(1)}, bf16[368,128]{1,0:T(8,128)(2,1)S(1)}, u32[]{:S(2)}, u32[]{:S(2)}) collective-permute-start(bf16[368,128]{1,0:T(8,128)(2,1)S(1)} %add.1.refs_0_), channel_id=1, source_target_pairs={{0,4},{1,5},{2,6},{3,7},{4,0},{5,1},{6,2},{7,3},{8,12},{9,13},{10,... | collective-permute-start | bytes 282632 | tf_op jit(solution)/shard_map/ppermute | solution.py:1318
  61.6 6.7 %collective-permute-start.6 = (bf16[368,128]{1,0:T(8,128)(2,1)S(1)}, bf16[368,128]{1,0:T(8,128)(2,1)S(1)}, u32[]{:S(2)}, u32[]{:S(2)}) collective-permute-start(bf16[368,128]{1,0:T(8,128)(2,1)S(1)} %add.1.refs_0_), channel_id=1, source_target_pairs={{0,3},{1,2},{2,1},{3,0},{4,7},{5,6},{6,5},{7,4},{8,11},{9,10},{10,... | collective-permute-start | bytes 282632 | tf_op jit(solution)/shard_map/ppermute | solution.py:1318
  63.3 5.4 %collective-permute-start.5 = (bf16[368,128]{1,0:T(8,128)(2,1)S(1)}, bf16[368,128]{1,0:T(8,128)(2,1)S(1)}, u32[]{:S(2)}, u32[]{:S(2)}) collective-permute-start(bf16[368,128]{1,0:T(8,128)(2,1)S(1)} %add.1.refs_0_), channel_id=1, source_target_pairs={{0,2},{1,3},{2,0},{3,1},{4,6},{5,7},{6,4},{7,5},{8,10},{9,11},{10,... | collective-permute-start | bytes 282632 | tf_op jit(solution)/shard_map/ppermute | solution.py:1318
  64.8 4.6 %collective-permute-start.4 = (bf16[368,128]{1,0:T(8,128)(2,1)S(1)}, bf16[368,128]{1,0:T(8,128)(2,1)S(1)}, u32[]{:S(2)}, u32[]{:S(2)}) collective-permute-start(bf16[368,128]{1,0:T(8,128)(2,1)S(1)} %add.1.refs_0_), channel_id=1, source_target_pairs={{0,1},{1,0},{2,3},{3,2},{4,5},{5,4},{6,7},{7,6},{8,9},{9,8},{10,11... | collective-permute-start | bytes 282632 | tf_op jit(solution)/shard_map/ppermute | solution.py:1318
  69.5 1.8 %collective-permute-start.11 = (bf16[4,368,128]{2,1,0:T(8,128)(2,1)S(1)}, bf16[4,368,128]{2,1,0:T(8,128)(2,1)S(1)}, u32[]{:S(2)}, u32[]{:S(2)}) collective-permute-start(bf16[4,368,128]{2,1,0:T(8,128)(2,1)S(1)} %get-tuple-element.77.one.refs_0_), channel_id=1, source_target_pairs={{0,16},{16,0},{1,17},{17,1},{2,18},{18,2},{3,19},{19,3},{4,20},{20... | collective-permute-start | bytes 1130504 | tf_op jit(solution)/shard_map/ppermute | solution.py:1307
  69.6 2.2 %collective-permute-start.12 = (bf16[4,368,128]{2,1,0:T(8,128)(2,1)S(1)}, bf16[4,368,128]{2,1,0:T(8,128)(2,1)S(1)}, u32[]{:S(2)}, u32[]{:S(2)}) collective-permute-start(bf16[4,368,128]{2,1,0:T(8,128)(2,1)S(1)} %get-tuple-element.78.two.refs_1_), channel_id=1, source_target_pairs={{0,16},{16,0},{1,17},{17,1},{2,18},{18,2},{3,19},{19,3},{4,20},{20... | collective-permute-start | bytes 1130504 | tf_op jit(solution)/shard_map/ppermute | solution.py:1307
where the time goes:
time: 73.8 us; the launch traced here: 73.2 us
  Pallas kernels  38.8 us (53%)
  starting transfers between devices  26.2 us (36%)
  waiting for transfers between devices  6.67 us (9%)
  between operations  1.58 us (2%)
    all_to_all x2, starting transfers between devices, exchanged(): lax.all_to_all(value, 'batch', split_axis=0, concat_axis=0, axis_index_gr...  13.3 us
    ppermute x8, starting transfers between devices, partner(): lax.ppermute(value, 'batch', [(b, b ^ distance) for b in range(count)])  11.6 us
    pallas_call x1, Pallas kernels, first(): pl.pallas_call(functools.partial(first_kernel, draw=draw), in_specs=[SCAL...  10.1 us
    pallas_call x1, Pallas kernels, plan(): pl.pallas_call(functools.partial(plan_kernel, per_pair=per_pair, depth=de...  8.49 us
    pallas_call x1, Pallas kernels, encode(): pl.pallas_call(encode_kernel, in_specs=[SCALARS, ANYWHERE, near, near, AN...  7.66 us
    ppermute x8, waiting for transfers between devices, partner(): lax.ppermute(value, 'batch', [(b, b ^ distance) for b in range(count)])  4.89 us
    pallas_call x1, Pallas kernels, pixels(): pl.pallas_call(functools.partial(pixels_kernel, start=start), in_specs=[S...  4.71 us
    pallas_call x1, Pallas kernels, back(): pl.pallas_call(back_kernel, in_specs=[near] * 6, out_shape=(shape_of(*pad...  2.65 us
  transfers between devices with their start and end apart: 15, of which 10 were waited for; matrix products, arithmetic and copies ran while one was open for 0% of the time, Pallas kernels for 37%

commit v1 on v0

--- a/solution.py
+++ b/solution.py
@@ -30,7 +30,8 @@
 )
 TABLE = 32
 CUBE = 8
-DRAW = 4
+DRAW = 3
+DRAW_ACROSS = 3
 SHORT = 16
 
 
@@ -68,7 +69,7 @@
 
 def soft(x):
     t = jnp.tanh(0.5 * x)
-    return jnp.maximum(x, 0.0) - jnp.log(0.5 + 0.5 * jnp.abs(t)), 0.5 + 0.5 * t
+    return jnp.maximum(x, 0.0) - jnp.log(0.5 + 0.5 * jnp.abs(t)), 1.0 + t
 
 
 def silu_pair(y):
@@ -305,7 +306,7 @@
     last_copies[0].wait()
     value, slope = soft(dot_rows(lw[...], h2[...]) + column(table[AT_LB, :]))
     enc[...] = value.astype(BF16)
-    s3[...] = slope
+    s3[...] = 0.5 * slope
     for g in range(steps):
         for copy in leaves(g):
             copy.wait()
@@ -603,6 +604,7 @@
     k2 = w2t.shape[0]
     inner = side // 2 - 1
     row_len = inner * k2
+    half_g3 = (0.5 * g3[...].astype(F32)).astype(BF16)
     tap, pix = iota((LANES, 256), 1), iota((LANES, 256), 0)
     for yrel in range(2):
         for p in range(3):
@@ -612,7 +614,8 @@
                 & (((tap >> 4) & 3) == ((pix >> 4) & 3) + 2 - 2 * p)
             )
             at = (yrel * 3 + p) * k2
-            t2[:, at : at + k2] = dot_lanes(hit.astype(F32).astype(BF16), w2t[...]).astype(BF16)
+            taps = dot_lanes(hit.astype(F32).astype(BF16), w2t[...])
+            t2[:, at : at + k2] = (0.5 * taps).astype(BF16)
     g2[0] = jnp.zeros(g2.shape[1:], BF16)
     g2[inner + 1] = jnp.zeros(g2.shape[1:], BF16)
     g1[0] = jnp.zeros(g1.shape[1:], BF16)
@@ -622,7 +625,7 @@
     total_two = jnp.zeros((k2, LANES), F32)
     for y in range(inner):
         at = slice(y * row_len, (y + 1) * row_len)
-        grad = dot(lw[at, :], g3[...]) * s2[at, :].astype(F32)
+        grad = dot(lw[at, :], half_g3) * s2[at, :].astype(F32)
         grad = grad.astype(BF16).reshape(inner, k2, LANES)
         g2[y + 1] = grad
         total_two = total_two + jnp.sum(grad.astype(F32), axis=0)
@@ -884,7 +887,7 @@
         if k >= members // 2:
             recv, here = recv_two, k - members // 2
         got = recv[here * size : (here + 1) * size, :]
-        out[k, 0:size, :] = (keep[at, :].astype(F32) + got.astype(F32)).astype(BF16)
+        out[k, 0:size, :] = keep[at, :] + got
         if k < members // 2:
             rows, span = c2_place(k)
             out[k, size:, :] = c2[rows, span].astype(BF16)
@@ -1406,15 +1409,17 @@
     while distance < peers:
         recv = partner(keep, distance)
         if distance == CUBE:
-            left = frames.shape[0] // 4 // STEP - DRAW
             frames_grad, token = pixels(
-                section, band, g1, other, keep, frames_grad, DRAW, left
+                section, band, g1, other, keep, frames_grad, DRAW, DRAW_ACROSS
             )
         distance *= 2
         keep = small_call(
             add_kernel, piece, (keep, recv), name="add", place=place, after=(token,)
         )
     parts = [keep] + [partner(keep, k) for k in range(1, CUBE)]
+    drawn = DRAW + DRAW_ACROSS
+    left = frames.shape[0] // 4 // STEP - drawn
+    frames_grad, token = pixels(section, band, g1, other, keep, frames_grad, drawn, left)
     got = small_call(
         relay_kernel,
         [bf16(CUBE // 2, *piece.shape)] * 2,
@@ -1422,6 +1427,7 @@
         [pltpu.VMEM((CUBE, *piece.shape), BF16)],
         name="relay",
         place=place,
+        after=(token,),
     )
     got_other = [swapped(v) for v in got]
     shapes = [p.shape for p in encoder_params + planner_params]

time: 73.8 us -> 73.3 us (level)
  waiting for transfers between devices: 6.67 us -> 4.41 us
  Pallas kernels: 38.8 us -> 40.8 us
    ppermute x8, waiting for transfers between devices: 4.89 us -> 1.91 us  [partner(): lax.ppermute(value, 'batch', [(b, b ^ distance) for b in range(count)])]
    pallas_call x1 -> x2, Pallas kernels: 4.71 us -> 7.47 us  [pixels(): pl.pallas_call(functools.partial(pixels_kernel, start=start), in_specs=[S...]
  transfers between devices with their start and end apart: 15 -> 15, of which waited for: 10 -> 7; matrix products, arithmetic and copies ran while one was open for 0% -> 0% of each run, Pallas kernels for 37% -> 40%
where the time goes in v1:
time: 73.3 us; the launch traced here: 72.7 us
  Pallas kernels  40.8 us (56%)
  starting transfers between devices  25.8 us (35%)
  waiting for transfers between devices  4.41 us (6%)
  between operations  1.62 us (2%)
    all_to_all x2, starting transfers between devices, exchanged(): lax.all_to_all(value, 'batch', split_axis=0, concat_axis=0, axis_index_gr...  13.1 us
    ppermute x8, starting transfers between devices, partner(): lax.ppermute(value, 'batch', [(b, b ^ distance) for b in range(count)])  11.4 us
    pallas_call x1, Pallas kernels, first(): pl.pallas_call(functools.partial(first_kernel, draw=draw), in_specs=[SCAL...  9.49 us
    pallas_call x1, Pallas kernels, plan(): pl.pallas_call(functools.partial(plan_kernel, per_pair=per_pair, depth=de...  8.49 us
    pallas_call x1, Pallas kernels, encode(): pl.pallas_call(encode_kernel, in_specs=[SCALARS, ANYWHERE, near, near, AN...  7.52 us
    pallas_call x2, Pallas kernels, pixels(): pl.pallas_call(functools.partial(pixels_kernel, start=start), in_specs=[S...  7.47 us
    pallas_call x1, Pallas kernels, back(): pl.pallas_call(back_kernel, in_specs=[near] * 6, out_shape=(shape_of(*pad...  2.63 us
    all_to_all x2, waiting for transfers between devices, exchanged(): lax.all_to_all(value, 'batch', split_axis=0, concat_axis=0, axis_index_gr...  2.01 us
  transfers between devices with their start and end apart: 15, of which 7 were waited for; matrix products, arithmetic and copies ran while one was open for 0% of the time, Pallas kernels for 40%

profile of v1, /device:TPU:0, one launch (start us, length us, event | category | flops | bytes accessed | tf_op | source)
XLA Modules:
  0.0 72.7 jit_solution(13771048341955525068)
XLA Ops:
  1.3 1.6 %numbers.1 = (f32[256,128]{1,0:T(8,128)}, f32[32,128]{1,0:T(8,128)S(1)}) custom-call(s32[3,256]{1,0:T(4,128)} %options.1, s32[1,256]{1,0:T(1,128)} %bitcast.38, f32[3,3,256]{2,1,0:T(4,128)} %targets.1, s32[1,256]{1,0:T(1,128)} %bitcast.39, f32[1,16]{1,0:T(1,128)} %bitcast.40, f32[1,32]{1,0:T(1,128)} %bitcast.41, f32[1,128]{1,0:T(1,128)} %bitcast.42, ...), custom_call_target="tpu_custom_call" | custom-call | flops 1100000000 | bytes 3600000 | tf_op jit(solution)/shard_map/numbers/pallas_call | solution.py:1361
  2.9 8.3 %all-to-all-start = ((f32[16,16,128]{2,1,0:T(8,128)}), f32[16,16,128]{2,1,0:T(8,128)S(1)}, u32[]{:S(2)}, u32[]{:S(2)}) async-start(f32[16,16,128]{2,1,0:T(8,128)} %bitcast.12), calls=%async_computation | async-start | bytes 262144 | tf_op jit(solution)/shard_map/all_to_all | solution.py:1314
  11.2 7.5 %encode.1 = (bf16[21,20,16,128]{3,2,1,0:T(8,128)(2,1)}, bf16[21,20,16,128]{3,2,1,0:T(8,128)(2,1)}, bf16[2592,128]{1,0:T(8,128)(2,1)}, bf16[2592,128]{1,0:T(8,128...) custom-call(s32[1]{0:T(128)} %bitcast.section, bf16[84,84,4,256]{3,2,1,0:T(4,128)(2,1)} %bitcast.32, ...), custom_call_target="tpu_custom_call" | custom-call | flops 9900000256 | bytes 32400000 | tf_op jit(solution)/shard_map/encode/pallas_call | solution.py:1143
  19.0 8.5 %plan.1 = (bf16[2560,128]{1,0:T(8,128)(2,1)S(1)}, bf16[1280,128]{1,0:T(8,128)(2,1)S(1)}, bf16[1280,128]{1,0:T(8,128)(2,1)S(1)}, f32[32,128]{1,0:T(8,128)S(1)}, bf16[128,128]{1,0:T(8,128)(2,1)S(1)}) custom-call(s32[1]{0:T(128)} %bitcast.section, f32[256,128]{1,0:T(8,128)S(1)} %bitcast.30, bf16[128,128]{1,0:T(8,128)(2,1)S(1)} %get-tuple-element.61.enc, ...), custom_call_target="tpu_custom_call" | custom-call | flops 12099999744 | bytes 39600000 | tf_op jit(solution)/shard_map/plan/pallas_call | solution.py:1190
  27.6 0.5 collective-permute-start.1
  28.1 2.6 %back.1 = (bf16[22,20,16,128]{3,2,1,0:T(8,128)(2,1)S(1)}, f32[32,256]{1,0:T(8,128)S(1)}, f32[8,128]{1,0:T(8,128)S(1)}) custom-call(bf16[128,128]{1,0:T(8,128)(2,1)S(1)} %get-tuple-element.68.g3, bf16[2592,128]{1,0:T(8,128)(2,1)S(1)} %copy-done, bf16[2592,128]{1,0:T(8,128)(2,1)S(1)} %copy-done.3, bf16[21,20,16,128]{3,2,1,0:T(8,128)(2,1)S(1)} %copy-done.2, ...), custom_call_target="tpu_custom_call" | custom-call | flops 27499999232 | bytes 90000000 | tf_op jit(solution)/shard_map/back/pallas_call | solution.py:1222
  30.9 0.9 %merge.1.after = bf16[8,336,128]{2,1,0:T(8,128)(2,1)} custom-call(bf16[2560,128]{1,0:T(8,128)(2,1)S(1)} %get-tuple-element.64.keep, bf16[1280,128]{1,0:T(8,128)(2,1)S(1)} %collective-permute-done.recv_one, bf16[1280,128]{1,0:T(8,128)(2,1)S(1)} %collective-permute-done.1.recv_two, f32[32,128]{1,0:T(8,128)S(1)} %get-tuple-element.67.small, ...), custom_call_target="tpu_custom_call" | custom-call | flops 32999999488 | bytes 108000000 | tf_op jit(solution)/shard_map/merge/pallas_call | solution.py:1291
  31.8 4.8 %all-to-all-start.1 = ((bf16[8,336,128]{2,1,0:T(8,128)(2,1)}), bf16[8,336,128]{2,1,0:T(8,128)(2,1)S(1)}, u32[]{:S(2)}, u32[]{:S(2)}) async-start(bf16[8,336,128]{2,1,0:T(8,128)(2,1)} %merge.1.after), calls=%async_computation.1 | async-start | bytes 1376256 | tf_op jit(solution)/shard_map/all_to_all | solution.py:1314
  36.6 9.5 %first.1 = (bf16[32,128]{1,0:T(8,128)(2,1)S(1)}, f32[84,84,2,256]{3,2,1,0:T(2,128)}, bf16[288,256]{1,0:T(8,128)(2,1)S(1)}) custom-call(s32[1]{0:T(128)} %bitcast.section, bf16[84,84,4,256]{3,2,1,0:T(4,128)(2,1)} %bitcast.33, bf16[22,20,16,128]{3,2,1,0:T(8,128)(2,1)S(1)} %get-tuple-element.74.g1.mine, bf16[16,256]{1,0:T(8,128)(2,1)} %bitcast.37, ...), custom_call_target="tpu_custom_call" | custom-call | flops 49500000256 | bytes 162000000 | tf_op jit(solution)/shard_map/first/pallas_call | solution.py:1241
  46.1 1.8 %all-to-all-done.1.got = bf16[8,336,128]{2,1,0:T(8,128)(2,1)S(1)} async-done(((bf16[8,336,128]{2,1,0:T(8,128)(2,1)}), bf16[8,336,128]{2,1,0:T(8,128)(2,1)S(1)}, u32[]{:S(2)}, u32[]{:S(2)}) %all-to-all-start.1) | async-done | bytes 688160 | tf_op jit(solution)/shard_map/all_to_all | solution.py:1314
  48.0 2.4 %collective-permute-start.3 = (bf16[368,128]{1,0:T(8,128)(2,1)S(1)}, bf16[368,128]{1,0:T(8,128)(2,1)S(1)}, u32[]{:S(2)}, u32[]{:S(2)}) collective-permute-start(bf16[368,128]{1,0:T(8,128)(2,1)S(1)} %cube.1.after.a), channel_id=1, source_target_pairs={{0,8},{1,9},{2,10},{3,11},{4,12},{5,13},{6,14},{7,15},{8,0},{9,1},... | collective-permute-start | bytes 282632 | tf_op jit(solution)/shard_map/ppermute | solution.py:1321
  50.4 4.7 %pixels.2 = (f32[84,84,2,256]{3,2,1,0:T(2,128)}, f32[8,128]{1,0:T(8,128)S(1)}) custom-call(s32[1]{0:T(128)} %bitcast.section, bf16[288,256]{1,0:T(8,128)(2,1)S(1)} %get-tuple-element.76.band, bf16[22,20,16,128]{3,2,1,0:T(8,128)(2,1)S(1)} %get-tuple-element.74.g1.mine, ...), custom_call_target="tpu_custom_call", output_to_operand_aliasing={{0}: (5, {})} | custom-call | flops 4070000128 | bytes 13320000 | tf_op jit(solution)/shard_map/pixels/pallas_call | solution.py:1267
  55.5 1.8 %collective-permute-start.10 = (bf16[368,128]{1,0:T(8,128)(2,1)S(1)}, bf16[368,128]{1,0:T(8,128)(2,1)S(1)}, u32[]{:S(2)}, u32[]{:S(2)}) collective-permute-start(bf16[368,128]{1,0:T(8,128)(2,1)S(1)} %add.1.after.refs_0_), channel_id=1, source_target_pairs={{0,7},{1,6},{2,5},{3,4},{4,3},{5,2},{6,1},{7,0},{8,15},{9,14},{10,... | collective-permute-start | bytes 282632 | tf_op jit(solution)/shard_map/ppermute | solution.py:1321
  57.3 1.3 %collective-permute-start.9 = (bf16[368,128]{1,0:T(8,128)(2,1)S(1)}, bf16[368,128]{1,0:T(8,128)(2,1)S(1)}, u32[]{:S(2)}, u32[]{:S(2)}) collective-permute-start(bf16[368,128]{1,0:T(8,128)(2,1)S(1)} %add.1.after.refs_0_), channel_id=1, source_target_pairs={{0,6},{1,7},{2,4},{3,5},{4,2},{5,3},{6,0},{7,1},{8,14},{9,15},{10,... | collective-permute-start | bytes 282632 | tf_op jit(solution)/shard_map/ppermute | solution.py:1321
  58.6 1.9 %collective-permute-start.8 = (bf16[368,128]{1,0:T(8,128)(2,1)S(1)}, bf16[368,128]{1,0:T(8,128)(2,1)S(1)}, u32[]{:S(2)}, u32[]{:S(2)}) collective-permute-start(bf16[368,128]{1,0:T(8,128)(2,1)S(1)} %add.1.after.refs_0_), channel_id=1, source_target_pairs={{0,5},{1,4},{2,7},{3,6},{4,1},{5,0},{6,3},{7,2},{8,13},{9,12},{10,... | collective-permute-start | bytes 282632 | tf_op jit(solution)/shard_map/ppermute | solution.py:1321
  60.5 0.9 %collective-permute-start.7 = (bf16[368,128]{1,0:T(8,128)(2,1)S(1)}, bf16[368,128]{1,0:T(8,128)(2,1)S(1)}, u32[]{:S(2)}, u32[]{:S(2)}) collective-permute-start(bf16[368,128]{1,0:T(8,128)(2,1)S(1)} %add.1.after.refs_0_), channel_id=1, source_target_pairs={{0,4},{1,5},{2,6},{3,7},{4,0},{5,1},{6,2},{7,3},{8,12},{9,13},{10,... | collective-permute-start | bytes 282632 | tf_op jit(solution)/shard_map/ppermute | solution.py:1321
  61.4 1.2 %collective-permute-start.6 = (bf16[368,128]{1,0:T(8,128)(2,1)S(1)}, bf16[368,128]{1,0:T(8,128)(2,1)S(1)}, u32[]{:S(2)}, u32[]{:S(2)}) collective-permute-start(bf16[368,128]{1,0:T(8,128)(2,1)S(1)} %add.1.after.refs_0_), channel_id=1, source_target_pairs={{0,3},{1,2},{2,1},{3,0},{4,7},{5,6},{6,5},{7,4},{8,11},{9,10},{10,... | collective-permute-start | bytes 282632 | tf_op jit(solution)/shard_map/ppermute | solution.py:1321
  62.9 0.7 collective-permute-start.5
  63.6 0.7 %collective-permute-done.9.refs_6_ = bf16[368,128]{1,0:T(8,128)(2,1)S(1)} collective-permute-done((bf16[368,128]{1,0:T(8,128)(2,1)S(1)}, bf16[368,128]{1,0:T(8,128)(2,1)S(1)}, u32[]{:S(2)}, u32[]{:S(2)}) %collective-permute-start.9) | collective-permute-done | bytes 94240 | tf_op jit(solution)/shard_map/ppermute | solution.py:1321
  64.3 1.3 %collective-permute-start.4 = (bf16[368,128]{1,0:T(8,128)(2,1)S(1)}, bf16[368,128]{1,0:T(8,128)(2,1)S(1)}, u32[]{:S(2)}, u32[]{:S(2)}) collective-permute-start(bf16[368,128]{1,0:T(8,128)(2,1)S(1)} %add.1.after.refs_0_), channel_id=1, source_target_pairs={{0,1},{1,0},{2,3},{3,2},{4,5},{5,4},{6,7},{7,6},{8,9},{9,8},{10,11... | collective-permute-start | bytes 282632 | tf_op jit(solution)/shard_map/ppermute | solution.py:1321
  65.6 2.8 %pixels.3 = (f32[84,84,2,256]{3,2,1,0:T(2,128)}, f32[8,128]{1,0:T(8,128)S(1)}) custom-call(s32[1]{0:T(128)} %bitcast.section, bf16[288,256]{1,0:T(8,128)(2,1)S(1)} %get-tuple-element.76.band, bf16[22,20,16,128]{3,2,1,0:T(8,128)(2,1)S(1)} %get-tuple-element.74.g1.mine, ...), custom_call_target="tpu_custom_call", output_to_operand_aliasing={{0}: (5, {})} | custom-call | flops 2090000000 | bytes 6840000 | tf_op jit(solution)/shard_map/pixels/pallas_call | solution.py:1267
  68.4 0.5 collective-permute-done.4.refs_1_
  69.6 1.2 %own.1 = (f32[2592,128]{1,0:T(8,128)}, f32[18,128,128]{2,1,0:T(8,128)}, f32[128,128]{1,0:T(8,128)}) custom-call(s32[1]{0:T(128)} %bitcast.section, bf16[4,368,128]{2,1,0:T(8,128)(2,1)S(1)} %get-tuple-element.81.one.refs_0_, bf16[4,368,128]{2,1,0:T(8,128)(2,1)S(1)} %get-tuple-element.82.two.refs_1_), custom_call_target="tpu_custom_call" | custom-call | flops 1100000000 | bytes 3600000 | tf_op jit(solution)/shard_map/own/pallas_call | solution.py:1443
  71.3 1.3 %unpack.1 = (f32[2592,128]{1,0:T(8,128)}, f32[18,128,128]{2,1,0:T(8,128)}, f32[128,128]{1,0:T(8,128)}, f32[1,1]{1,0:T(1,128)}, f32[16,256]{1,0:T(8,128)}, /*inde...) custom-call(s32[1]{0:T(128)} %bitcast.section, ...), custom_call_target="tpu_custom_call", output_to_operand_aliasing={{0}: (5, {}), {1}: (6, {}), {2}: (7, {})} | custom-call | flops 1650000000 | bytes 5400000 | tf_op jit(solution)/shard_map/unpack/pallas_call | solution.py:1453
  (27 shorter events, 2.5 us)
Async XLA Ops:
  2.9 16.1 %all-to-all-start = ((f32[16,16,128]{2,1,0:T(8,128)}), f32[16,16,128]{2,1,0:T(8,128)S(1)}, u32[]{:S(2)}, u32[]{:S(2)}) async-start(f32[16,16,128]{2,1,0:T(8,128)} %bitcast.12), calls=%async_computation | async-start | bytes 262144 | tf_op jit(solution)/shard_map/all_to_all | solution.py:1314
  19.0 9.1 %copy-start = (bf16[2592,128]{1,0:T(8,128)(2,1)S(1)}, bf16[2592,128]{1,0:T(8,128)(2,1)}, u32[]{:S(2)}) copy-start(bf16[2592,128]{1,0:T(8,128)(2,1)} %lw.1) | copy-start | bytes 1990660
  19.0 9.1 %copy-start.1 = (bf16[21,20,16,128]{3,2,1,0:T(8,128)(2,1)S(1)}, bf16[21,20,16,128]{3,2,1,0:T(8,128)(2,1)}, u32[]{:S(2)}) copy-start(bf16[21,20,16,128]{3,2,1,0:T(8,128)(2,1)} %get-tuple-element.71.h1) | copy-start | bytes 5160964
  19.0 9.1 %copy-start.2 = (bf16[21,20,16,128]{3,2,1,0:T(8,128)(2,1)S(1)}, bf16[21,20,16,128]{3,2,1,0:T(8,128)(2,1)}, u32[]{:S(2)}) copy-start(bf16[21,20,16,128]{3,2,1,0:T(8,128)(2,1)} %get-tuple-element.70.s1) | copy-start | bytes 5160964
  19.0 9.1 %copy-start.3 = (bf16[2592,128]{1,0:T(8,128)(2,1)S(1)}, bf16[2592,128]{1,0:T(8,128)(2,1)}, u32[]{:S(2)}) copy-start(bf16[2592,128]{1,0:T(8,128)(2,1)} %get-tuple-element.69.s2) | copy-start | bytes 1990660
  27.5 3.4 %collective-permute-start = (bf16[1280,128]{1,0:T(8,128)(2,1)S(1)}, bf16[1280,128]{1,0:T(8,128)(2,1)S(1)}, u32[]{:S(2)}, u32[]{:S(2)}) collective-permute-start(bf16[1280,128]{1,0:T(8,128)(2,1)S(1)} %get-tuple-element.65), channel_id=1, source_target_pairs={{0,16},{16,0},{1,17},{17,1},{2,18},{18,2},{3,19},{19,3},{4,20},{20... | collective-permute-start | bytes 983048 | tf_op jit(solution)/shard_map/ppermute | solution.py:1310
  27.6 3.3 %collective-permute-start.1 = (bf16[1280,128]{1,0:T(8,128)(2,1)S(1)}, bf16[1280,128]{1,0:T(8,128)(2,1)S(1)}, u32[]{:S(2)}, u32[]{:S(2)}) collective-permute-start(bf16[1280,128]{1,0:T(8,128)(2,1)S(1)} %get-tuple-element.66), channel_id=1, source_target_pairs={{0,16},{16,0},{1,17},{17,1},{2,18},{18,2},{3,19},{19,3},{4,20},{20... | collective-permute-start | bytes 983048 | tf_op jit(solution)/shard_map/ppermute | solution.py:1310
  30.7 5.9 %collective-permute-start.2 = (bf16[22,20,16,128]{3,2,1,0:T(8,128)(2,1)S(1)}, bf16[22,20,16,128]{3,2,1,0:T(8,128)(2,1)}, u32[]{:S(2)}, u32[]{:S(2)}) collective-permute-start(bf16[22,20,16,128]{3,2,1,0:T(8,128)(2,1)S(1)} %get-tuple-element.74.g1.mine), channel_id=1, source_target_pairs={{0,16},{16,0},{1,17},{17,1},{2,18},{18,2},{3,19},{19,3},{4,20},{20... | collective-permute-start | bytes 5406728 | tf_op jit(solution)/shard_map/ppermute | solution.py:1310
  31.8 16.1 %all-to-all-start.1 = ((bf16[8,336,128]{2,1,0:T(8,128)(2,1)}), bf16[8,336,128]{2,1,0:T(8,128)(2,1)S(1)}, u32[]{:S(2)}, u32[]{:S(2)}) async-start(bf16[8,336,128]{2,1,0:T(8,128)(2,1)} %merge.1.after), calls=%async_computation.1 | async-start | bytes 1376256 | tf_op jit(solution)/shard_map/all_to_all | solution.py:1314
  48.0 7.5 %collective-permute-start.3 = (bf16[368,128]{1,0:T(8,128)(2,1)S(1)}, bf16[368,128]{1,0:T(8,128)(2,1)S(1)}, u32[]{:S(2)}, u32[]{:S(2)}) collective-permute-start(bf16[368,128]{1,0:T(8,128)(2,1)S(1)} %cube.1.after.a), channel_id=1, source_target_pairs={{0,8},{1,9},{2,10},{3,11},{4,12},{5,13},{6,14},{7,15},{8,0},{9,1},... | collective-permute-start | bytes 282632 | tf_op jit(solution)/shard_map/ppermute | solution.py:1321
  55.5 7.4 %collective-permute-start.10 = (bf16[368,128]{1,0:T(8,128)(2,1)S(1)}, bf16[368,128]{1,0:T(8,128)(2,1)S(1)}, u32[]{:S(2)}, u32[]{:S(2)}) collective-permute-start(bf16[368,128]{1,0:T(8,128)(2,1)S(1)} %add.1.after.refs_0_), channel_id=1, source_target_pairs={{0,7},{1,6},{2,5},{3,4},{4,3},{5,2},{6,1},{7,0},{8,15},{9,14},{10,... | collective-permute-start | bytes 282632 | tf_op jit(solution)/shard_map/ppermute | solution.py:1321
  57.3 7.0 %collective-permute-start.9 = (bf16[368,128]{1,0:T(8,128)(2,1)S(1)}, bf16[368,128]{1,0:T(8,128)(2,1)S(1)}, u32[]{:S(2)}, u32[]{:S(2)}) collective-permute-start(bf16[368,128]{1,0:T(8,128)(2,1)S(1)} %add.1.after.refs_0_), channel_id=1, source_target_pairs={{0,6},{1,7},{2,4},{3,5},{4,2},{5,3},{6,0},{7,1},{8,14},{9,15},{10,... | collective-permute-start | bytes 282632 | tf_op jit(solution)/shard_map/ppermute | solution.py:1321
  58.6 9.7 %collective-permute-start.8 = (bf16[368,128]{1,0:T(8,128)(2,1)S(1)}, bf16[368,128]{1,0:T(8,128)(2,1)S(1)}, u32[]{:S(2)}, u32[]{:S(2)}) collective-permute-start(bf16[368,128]{1,0:T(8,128)(2,1)S(1)} %add.1.after.refs_0_), channel_id=1, source_target_pairs={{0,5},{1,4},{2,7},{3,6},{4,1},{5,0},{6,3},{7,2},{8,13},{9,12},{10,... | collective-permute-start | bytes 282632 | tf_op jit(solution)/shard_map/ppermute | solution.py:1321
  60.5 7.8 %collective-permute-start.7 = (bf16[368,128]{1,0:T(8,128)(2,1)S(1)}, bf16[368,128]{1,0:T(8,128)(2,1)S(1)}, u32[]{:S(2)}, u32[]{:S(2)}) collective-permute-start(bf16[368,128]{1,0:T(8,128)(2,1)S(1)} %add.1.after.refs_0_), channel_id=1, source_target_pairs={{0,4},{1,5},{2,6},{3,7},{4,0},{5,1},{6,2},{7,3},{8,12},{9,13},{10,... | collective-permute-start | bytes 282632 | tf_op jit(solution)/shard_map/ppermute | solution.py:1321
  61.4 6.9 %collective-permute-start.6 = (bf16[368,128]{1,0:T(8,128)(2,1)S(1)}, bf16[368,128]{1,0:T(8,128)(2,1)S(1)}, u32[]{:S(2)}, u32[]{:S(2)}) collective-permute-start(bf16[368,128]{1,0:T(8,128)(2,1)S(1)} %add.1.after.refs_0_), channel_id=1, source_target_pairs={{0,3},{1,2},{2,1},{3,0},{4,7},{5,6},{6,5},{7,4},{8,11},{9,10},{10,... | collective-permute-start | bytes 282632 | tf_op jit(solution)/shard_map/ppermute | solution.py:1321
  62.9 5.5 %collective-permute-start.5 = (bf16[368,128]{1,0:T(8,128)(2,1)S(1)}, bf16[368,128]{1,0:T(8,128)(2,1)S(1)}, u32[]{:S(2)}, u32[]{:S(2)}) collective-permute-start(bf16[368,128]{1,0:T(8,128)(2,1)S(1)} %add.1.after.refs_0_), channel_id=1, source_target_pairs={{0,2},{1,3},{2,0},{3,1},{4,6},{5,7},{6,4},{7,5},{8,10},{9,11},{10,... | collective-permute-start | bytes 282632 | tf_op jit(solution)/shard_map/ppermute | solution.py:1321
  64.3 4.6 %collective-permute-start.4 = (bf16[368,128]{1,0:T(8,128)(2,1)S(1)}, bf16[368,128]{1,0:T(8,128)(2,1)S(1)}, u32[]{:S(2)}, u32[]{:S(2)}) collective-permute-start(bf16[368,128]{1,0:T(8,128)(2,1)S(1)} %add.1.after.refs_0_), channel_id=1, source_target_pairs={{0,1},{1,0},{2,3},{3,2},{4,5},{5,4},{6,7},{7,6},{8,9},{9,8},{10,11... | collective-permute-start | bytes 282632 | tf_op jit(solution)/shard_map/ppermute | solution.py:1321
  69.0 1.8 %collective-permute-start.11 = (bf16[4,368,128]{2,1,0:T(8,128)(2,1)S(1)}, bf16[4,368,128]{2,1,0:T(8,128)(2,1)S(1)}, u32[]{:S(2)}, u32[]{:S(2)}) collective-permute-start(bf16[4,368,128]{2,1,0:T(8,128)(2,1)S(1)} %get-tuple-element.81.one.refs_0_), channel_id=1, source_target_pairs={{0,16},{16,0},{1,17},{17,1},{2,18},{18,2},{3,19},{19,3},{4,20},{20... | collective-permute-start | bytes 1130504 | tf_op jit(solution)/shard_map/ppermute | solution.py:1310
  69.1 2.2 %collective-permute-start.12 = (bf16[4,368,128]{2,1,0:T(8,128)(2,1)S(1)}, bf16[4,368,128]{2,1,0:T(8,128)(2,1)S(1)}, u32[]{:S(2)}, u32[]{:S(2)}) collective-permute-start(bf16[4,368,128]{2,1,0:T(8,128)(2,1)S(1)} %get-tuple-element.82.two.refs_1_), channel_id=1, source_target_pairs={{0,16},{16,0},{1,17},{17,1},{2,18},{18,2},{3,19},{19,3},{4,20},{20... | collective-permute-start | bytes 1130504 | tf_op jit(solution)/shard_map/ppermute | solution.py:1310

commit v2 on v1

--- a/solution.py
+++ b/solution.py
@@ -30,6 +30,7 @@
 )
 TABLE = 32
 CUBE = 8
+TURNS = (0, 4, 3, 2, 5, 1, 6, 7)
 DRAW = 3
 DRAW_ACROSS = 3
 SHORT = 16
@@ -932,7 +933,7 @@
 def relay_kernel(batch, *refs):
     parts, (one, two, out) = refs[:CUBE], refs[-3:]
     me = batch[0] % CUBE
-    for k, part in enumerate(parts):
+    for k, part in zip(TURNS, parts):
         out[me ^ k] = part[...]
     one[...] = out[: CUBE // 2]
     two[...] = out[CUBE // 2 :]
@@ -1416,7 +1417,7 @@
         keep = small_call(
             add_kernel, piece, (keep, recv), name="add", place=place, after=(token,)
         )
-    parts = [keep] + [partner(keep, k) for k in range(1, CUBE)]
+    parts = [partner(keep, k) if k else keep for k in TURNS]
     drawn = DRAW + DRAW_ACROSS
     left = frames.shape[0] // 4 // STEP - drawn
     frames_grad, token = pixels(section, band, g1, other, keep, frames_grad, drawn, left)

time: 73.3 us -> 73.4 us (level)
  no operation moved by 1% of the time
where the time goes in v2:
time: 73.4 us; the launch traced here: 72.8 us
  Pallas kernels  40.8 us (56%)
  starting transfers between devices  26.1 us (36%)
  waiting for transfers between devices  4.22 us (6%)
  between operations  1.61 us (2%)
    all_to_all x2, starting transfers between devices, exchanged(): lax.all_to_all(value, 'batch', split_axis=0, concat_axis=0, axis_index_gr...  13.1 us
    ppermute x8, starting transfers between devices, partner(): lax.ppermute(value, 'batch', [(b, b ^ distance) for b in range(count)])  11.7 us
    pallas_call x1, Pallas kernels, first(): pl.pallas_call(functools.partial(first_kernel, draw=draw), in_specs=[SCAL...  9.49 us
    pallas_call x1, Pallas kernels, plan(): pl.pallas_call(functools.partial(plan_kernel, per_pair=per_pair, depth=de...  8.49 us
    pallas_call x1, Pallas kernels, encode(): pl.pallas_call(encode_kernel, in_specs=[SCALARS, ANYWHERE, near, near, AN...  7.52 us
    pallas_call x2, Pallas kernels, pixels(): pl.pallas_call(functools.partial(pixels_kernel, start=start), in_specs=[S...  7.47 us
    pallas_call x1, Pallas kernels, back(): pl.pallas_call(back_kernel, in_specs=[near] * 6, out_shape=(shape_of(*pad...  2.63 us
    all_to_all x2, waiting for transfers between devices, exchanged(): lax.all_to_all(value, 'batch', split_axis=0, concat_axis=0, axis_index_gr...  2.01 us
  transfers between devices with their start and end apart: 15, of which 7 were waited for; matrix products, arithmetic and copies ran while one was open for 0% of the time, Pallas kernels for 40%

profile of v2, /device:TPU:0, one launch (start us, length us, event | category | flops | bytes accessed | tf_op | source)
XLA Modules:
  0.0 72.8 jit_solution(3654727833901907344)
XLA Ops:
  1.3 1.6 %numbers.1 = (f32[256,128]{1,0:T(8,128)}, f32[32,128]{1,0:T(8,128)S(1)}) custom-call(s32[3,256]{1,0:T(4,128)} %options.1, s32[1,256]{1,0:T(1,128)} %bitcast.38, f32[3,3,256]{2,1,0:T(4,128)} %targets.1, s32[1,256]{1,0:T(1,128)} %bitcast.39, f32[1,16]{1,0:T(1,128)} %bitcast.40, f32[1,32]{1,0:T(1,128)} %bitcast.41, f32[1,128]{1,0:T(1,128)} %bitcast.42, ...), custom_call_target="tpu_custom_call" | custom-call | flops 1100000000 | bytes 3600000 | tf_op jit(solution)/shard_map/numbers/pallas_call | solution.py:1362
  2.9 8.3 %all-to-all-start = ((f32[16,16,128]{2,1,0:T(8,128)}), f32[16,16,128]{2,1,0:T(8,128)S(1)}, u32[]{:S(2)}, u32[]{:S(2)}) async-start(f32[16,16,128]{2,1,0:T(8,128)} %bitcast.12), calls=%async_computation | async-start | bytes 262144 | tf_op jit(solution)/shard_map/all_to_all | solution.py:1315
  11.2 7.5 %encode.1 = (bf16[21,20,16,128]{3,2,1,0:T(8,128)(2,1)}, bf16[21,20,16,128]{3,2,1,0:T(8,128)(2,1)}, bf16[2592,128]{1,0:T(8,128)(2,1)}, bf16[2592,128]{1,0:T(8,128...) custom-call(s32[1]{0:T(128)} %bitcast.section, bf16[84,84,4,256]{3,2,1,0:T(4,128)(2,1)} %bitcast.32, ...), custom_call_target="tpu_custom_call" | custom-call | flops 9900000256 | bytes 32400000 | tf_op jit(solution)/shard_map/encode/pallas_call | solution.py:1144
  19.0 8.5 %plan.1 = (bf16[2560,128]{1,0:T(8,128)(2,1)S(1)}, bf16[1280,128]{1,0:T(8,128)(2,1)S(1)}, bf16[1280,128]{1,0:T(8,128)(2,1)S(1)}, f32[32,128]{1,0:T(8,128)S(1)}, bf16[128,128]{1,0:T(8,128)(2,1)S(1)}) custom-call(s32[1]{0:T(128)} %bitcast.section, f32[256,128]{1,0:T(8,128)S(1)} %bitcast.30, bf16[128,128]{1,0:T(8,128)(2,1)S(1)} %get-tuple-element.61.enc, ...), custom_call_target="tpu_custom_call" | custom-call | flops 12099999744 | bytes 39600000 | tf_op jit(solution)/shard_map/plan/pallas_call | solution.py:1191
  27.6 0.5 collective-permute-start.1
  28.1 2.6 %back.1 = (bf16[22,20,16,128]{3,2,1,0:T(8,128)(2,1)S(1)}, f32[32,256]{1,0:T(8,128)S(1)}, f32[8,128]{1,0:T(8,128)S(1)}) custom-call(bf16[128,128]{1,0:T(8,128)(2,1)S(1)} %get-tuple-element.68.g3, bf16[2592,128]{1,0:T(8,128)(2,1)S(1)} %copy-done, bf16[2592,128]{1,0:T(8,128)(2,1)S(1)} %copy-done.3, bf16[21,20,16,128]{3,2,1,0:T(8,128)(2,1)S(1)} %copy-done.2, ...), custom_call_target="tpu_custom_call" | custom-call | flops 27499999232 | bytes 90000000 | tf_op jit(solution)/shard_map/back/pallas_call | solution.py:1223
  30.9 0.9 %merge.1.after = bf16[8,336,128]{2,1,0:T(8,128)(2,1)} custom-call(bf16[2560,128]{1,0:T(8,128)(2,1)S(1)} %get-tuple-element.64.keep, bf16[1280,128]{1,0:T(8,128)(2,1)S(1)} %collective-permute-done.recv_one, bf16[1280,128]{1,0:T(8,128)(2,1)S(1)} %collective-permute-done.1.recv_two, f32[32,128]{1,0:T(8,128)S(1)} %get-tuple-element.67.small, ...), custom_call_target="tpu_custom_call" | custom-call | flops 32999999488 | bytes 108000000 | tf_op jit(solution)/shard_map/merge/pallas_call | solution.py:1292
  31.8 4.8 %all-to-all-start.1 = ((bf16[8,336,128]{2,1,0:T(8,128)(2,1)}), bf16[8,336,128]{2,1,0:T(8,128)(2,1)S(1)}, u32[]{:S(2)}, u32[]{:S(2)}) async-start(bf16[8,336,128]{2,1,0:T(8,128)(2,1)} %merge.1.after), calls=%async_computation.1 | async-start | bytes 1376256 | tf_op jit(solution)/shard_map/all_to_all | solution.py:1315
  36.6 9.5 %first.1 = (bf16[32,128]{1,0:T(8,128)(2,1)S(1)}, f32[84,84,2,256]{3,2,1,0:T(2,128)}, bf16[288,256]{1,0:T(8,128)(2,1)S(1)}) custom-call(s32[1]{0:T(128)} %bitcast.section, bf16[84,84,4,256]{3,2,1,0:T(4,128)(2,1)} %bitcast.33, bf16[22,20,16,128]{3,2,1,0:T(8,128)(2,1)S(1)} %get-tuple-element.74.g1.mine, bf16[16,256]{1,0:T(8,128)(2,1)} %bitcast.37, ...), custom_call_target="tpu_custom_call" | custom-call | flops 49500000256 | bytes 162000000 | tf_op jit(solution)/shard_map/first/pallas_call | solution.py:1242
  46.1 1.8 %all-to-all-done.1.got = bf16[8,336,128]{2,1,0:T(8,128)(2,1)S(1)} async-done(((bf16[8,336,128]{2,1,0:T(8,128)(2,1)}), bf16[8,336,128]{2,1,0:T(8,128)(2,1)S(1)}, u32[]{:S(2)}, u32[]{:S(2)}) %all-to-all-start.1) | async-done | bytes 688160 | tf_op jit(solution)/shard_map/all_to_all | solution.py:1315
  48.0 2.4 %collective-permute-start.3 = (bf16[368,128]{1,0:T(8,128)(2,1)S(1)}, bf16[368,128]{1,0:T(8,128)(2,1)S(1)}, u32[]{:S(2)}, u32[]{:S(2)}) collective-permute-start(bf16[368,128]{1,0:T(8,128)(2,1)S(1)} %cube.1.after.a), channel_id=1, source_target_pairs={{0,8},{1,9},{2,10},{3,11},{4,12},{5,13},{6,14},{7,15},{8,0},{9,1},... | collective-permute-start | bytes 282632 | tf_op jit(solution)/shard_map/ppermute | solution.py:1322
  50.4 4.7 %pixels.2 = (f32[84,84,2,256]{3,2,1,0:T(2,128)}, f32[8,128]{1,0:T(8,128)S(1)}) custom-call(s32[1]{0:T(128)} %bitcast.section, bf16[288,256]{1,0:T(8,128)(2,1)S(1)} %get-tuple-element.76.band, bf16[22,20,16,128]{3,2,1,0:T(8,128)(2,1)S(1)} %get-tuple-element.74.g1.mine, ...), custom_call_target="tpu_custom_call", output_to_operand_aliasing={{0}: (5, {})} | custom-call | flops 4070000128 | bytes 13320000 | tf_op jit(solution)/shard_map/pixels/pallas_call | solution.py:1268
  55.5 1.8 %collective-permute-start.10 = (bf16[368,128]{1,0:T(8,128)(2,1)S(1)}, bf16[368,128]{1,0:T(8,128)(2,1)S(1)}, u32[]{:S(2)}, u32[]{:S(2)}) collective-permute-start(bf16[368,128]{1,0:T(8,128)(2,1)S(1)} %add.1.after.refs_0_), channel_id=1, source_target_pairs={{0,7},{1,6},{2,5},{3,4},{4,3},{5,2},{6,1},{7,0},{8,15},{9,14},{10,... | collective-permute-start | bytes 282632 | tf_op jit(solution)/shard_map/ppermute | solution.py:1322
  57.3 1.3 %collective-permute-start.9 = (bf16[368,128]{1,0:T(8,128)(2,1)S(1)}, bf16[368,128]{1,0:T(8,128)(2,1)S(1)}, u32[]{:S(2)}, u32[]{:S(2)}) collective-permute-start(bf16[368,128]{1,0:T(8,128)(2,1)S(1)} %add.1.after.refs_0_), channel_id=1, source_target_pairs={{0,6},{1,7},{2,4},{3,5},{4,2},{5,3},{6,0},{7,1},{8,14},{9,15},{10,... | collective-permute-start | bytes 282632 | tf_op jit(solution)/shard_map/ppermute | solution.py:1322
  58.6 1.4 %collective-permute-start.8 = (bf16[368,128]{1,0:T(8,128)(2,1)S(1)}, bf16[368,128]{1,0:T(8,128)(2,1)S(1)}, u32[]{:S(2)}, u32[]{:S(2)}) collective-permute-start(bf16[368,128]{1,0:T(8,128)(2,1)S(1)} %add.1.after.refs_0_), channel_id=1, source_target_pairs={{0,1},{1,0},{2,3},{3,2},{4,5},{5,4},{6,7},{7,6},{8,9},{9,8},{10,11... | collective-permute-start | bytes 282632 | tf_op jit(solution)/shard_map/ppermute | solution.py:1322
  60.0 1.1 %collective-permute-start.7 = (bf16[368,128]{1,0:T(8,128)(2,1)S(1)}, bf16[368,128]{1,0:T(8,128)(2,1)S(1)}, u32[]{:S(2)}, u32[]{:S(2)}) collective-permute-start(bf16[368,128]{1,0:T(8,128)(2,1)S(1)} %add.1.after.refs_0_), channel_id=1, source_target_pairs={{0,5},{1,4},{2,7},{3,6},{4,1},{5,0},{6,3},{7,2},{8,13},{9,12},{10,... | collective-permute-start | bytes 282632 | tf_op jit(solution)/shard_map/ppermute | solution.py:1322
  61.1 1.2 %collective-permute-start.6 = (bf16[368,128]{1,0:T(8,128)(2,1)S(1)}, bf16[368,128]{1,0:T(8,128)(2,1)S(1)}, u32[]{:S(2)}, u32[]{:S(2)}) collective-permute-start(bf16[368,128]{1,0:T(8,128)(2,1)S(1)} %add.1.after.refs_0_), channel_id=1, source_target_pairs={{0,2},{1,3},{2,0},{3,1},{4,6},{5,7},{6,4},{7,5},{8,10},{9,11},{10,... | collective-permute-start | bytes 282632 | tf_op jit(solution)/shard_map/ppermute | solution.py:1322
  62.3 0.7 %collective-permute-done.10.refs_7_ = bf16[368,128]{1,0:T(8,128)(2,1)S(1)} collective-permute-done((bf16[368,128]{1,0:T(8,128)(2,1)S(1)}, bf16[368,128]{1,0:T(8,128)(2,1)S(1)}, u32[]{:S(2)}, u32[]{:S(2)}) %collective-permute-start.10) | collective-permute-done | bytes 94240 | tf_op jit(solution)/shard_map/ppermute | solution.py:1322
  63.0 1.4 %collective-permute-start.5 = (bf16[368,128]{1,0:T(8,128)(2,1)S(1)}, bf16[368,128]{1,0:T(8,128)(2,1)S(1)}, u32[]{:S(2)}, u32[]{:S(2)}) collective-permute-start(bf16[368,128]{1,0:T(8,128)(2,1)S(1)} %add.1.after.refs_0_), channel_id=1, source_target_pairs={{0,3},{1,2},{2,1},{3,0},{4,7},{5,6},{6,5},{7,4},{8,11},{9,10},{10,... | collective-permute-start | bytes 282632 | tf_op jit(solution)/shard_map/ppermute | solution.py:1322
  64.4 1.2 %collective-permute-start.4 = (bf16[368,128]{1,0:T(8,128)(2,1)S(1)}, bf16[368,128]{1,0:T(8,128)(2,1)S(1)}, u32[]{:S(2)}, u32[]{:S(2)}) collective-permute-start(bf16[368,128]{1,0:T(8,128)(2,1)S(1)} %add.1.after.refs_0_), channel_id=1, source_target_pairs={{0,4},{1,5},{2,6},{3,7},{4,0},{5,1},{6,2},{7,3},{8,12},{9,13},{10,... | collective-permute-start | bytes 282632 | tf_op jit(solution)/shard_map/ppermute | solution.py:1322
  65.5 2.8 %pixels.3 = (f32[84,84,2,256]{3,2,1,0:T(2,128)}, f32[8,128]{1,0:T(8,128)S(1)}) custom-call(s32[1]{0:T(128)} %bitcast.section, bf16[288,256]{1,0:T(8,128)(2,1)S(1)} %get-tuple-element.76.band, bf16[22,20,16,128]{3,2,1,0:T(8,128)(2,1)S(1)} %get-tuple-element.74.g1.mine, ...), custom_call_target="tpu_custom_call", output_to_operand_aliasing={{0}: (5, {})} | custom-call | flops 2090000000 | bytes 6840000 | tf_op jit(solution)/shard_map/pixels/pallas_call | solution.py:1268
  69.1 0.5 collective-permute-start.12
  69.6 1.2 %own.1 = (f32[2592,128]{1,0:T(8,128)}, f32[18,128,128]{2,1,0:T(8,128)}, f32[128,128]{1,0:T(8,128)}) custom-call(s32[1]{0:T(128)} %bitcast.section, bf16[4,368,128]{2,1,0:T(8,128)(2,1)S(1)} %get-tuple-element.81.one.refs_0_, bf16[4,368,128]{2,1,0:T(8,128)(2,1)S(1)} %get-tuple-element.82.two.refs_1_), custom_call_target="tpu_custom_call" | custom-call | flops 1100000000 | bytes 3600000 | tf_op jit(solution)/shard_map/own/pallas_call | solution.py:1444
  71.4 1.3 %unpack.1 = (f32[2592,128]{1,0:T(8,128)}, f32[18,128,128]{2,1,0:T(8,128)}, f32[128,128]{1,0:T(8,128)}, f32[1,1]{1,0:T(1,128)}, f32[16,256]{1,0:T(8,128)}, /*inde...) custom-call(s32[1]{0:T(128)} %bitcast.section, ...), custom_call_target="tpu_custom_call", output_to_operand_aliasing={{0}: (5, {}), {1}: (6, {}), {2}: (7, {})} | custom-call | flops 1650000000 | bytes 5400000 | tf_op jit(solution)/shard_map/unpack/pallas_call | solution.py:1454
  (27 shorter events, 2.3 us)
Async XLA Ops:
  2.9 16.1 %all-to-all-start = ((f32[16,16,128]{2,1,0:T(8,128)}), f32[16,16,128]{2,1,0:T(8,128)S(1)}, u32[]{:S(2)}, u32[]{:S(2)}) async-start(f32[16,16,128]{2,1,0:T(8,128)} %bitcast.12), calls=%async_computation | async-start | bytes 262144 | tf_op jit(solution)/shard_map/all_to_all | solution.py:1315
  19.0 9.1 %copy-start = (bf16[2592,128]{1,0:T(8,128)(2,1)S(1)}, bf16[2592,128]{1,0:T(8,128)(2,1)}, u32[]{:S(2)}) copy-start(bf16[2592,128]{1,0:T(8,128)(2,1)} %lw.1) | copy-start | bytes 1990660
  19.0 9.1 %copy-start.1 = (bf16[21,20,16,128]{3,2,1,0:T(8,128)(2,1)S(1)}, bf16[21,20,16,128]{3,2,1,0:T(8,128)(2,1)}, u32[]{:S(2)}) copy-start(bf16[21,20,16,128]{3,2,1,0:T(8,128)(2,1)} %get-tuple-element.71.h1) | copy-start | bytes 5160964
  19.0 9.1 %copy-start.2 = (bf16[21,20,16,128]{3,2,1,0:T(8,128)(2,1)S(1)}, bf16[21,20,16,128]{3,2,1,0:T(8,128)(2,1)}, u32[]{:S(2)}) copy-start(bf16[21,20,16,128]{3,2,1,0:T(8,128)(2,1)} %get-tuple-element.70.s1) | copy-start | bytes 5160964
  19.0 9.1 %copy-start.3 = (bf16[2592,128]{1,0:T(8,128)(2,1)S(1)}, bf16[2592,128]{1,0:T(8,128)(2,1)}, u32[]{:S(2)}) copy-start(bf16[2592,128]{1,0:T(8,128)(2,1)} %get-tuple-element.69.s2) | copy-start | bytes 1990660
  27.5 3.4 %collective-permute-start = (bf16[1280,128]{1,0:T(8,128)(2,1)S(1)}, bf16[1280,128]{1,0:T(8,128)(2,1)S(1)}, u32[]{:S(2)}, u32[]{:S(2)}) collective-permute-start(bf16[1280,128]{1,0:T(8,128)(2,1)S(1)} %get-tuple-element.65), channel_id=1, source_target_pairs={{0,16},{16,0},{1,17},{17,1},{2,18},{18,2},{3,19},{19,3},{4,20},{20... | collective-permute-start | bytes 983048 | tf_op jit(solution)/shard_map/ppermute | solution.py:1311
  27.6 3.3 %collective-permute-start.1 = (bf16[1280,128]{1,0:T(8,128)(2,1)S(1)}, bf16[1280,128]{1,0:T(8,128)(2,1)S(1)}, u32[]{:S(2)}, u32[]{:S(2)}) collective-permute-start(bf16[1280,128]{1,0:T(8,128)(2,1)S(1)} %get-tuple-element.66), channel_id=1, source_target_pairs={{0,16},{16,0},{1,17},{17,1},{2,18},{18,2},{3,19},{19,3},{4,20},{20... | collective-permute-start | bytes 983048 | tf_op jit(solution)/shard_map/ppermute | solution.py:1311
  30.7 5.9 %collective-permute-start.2 = (bf16[22,20,16,128]{3,2,1,0:T(8,128)(2,1)S(1)}, bf16[22,20,16,128]{3,2,1,0:T(8,128)(2,1)}, u32[]{:S(2)}, u32[]{:S(2)}) collective-permute-start(bf16[22,20,16,128]{3,2,1,0:T(8,128)(2,1)S(1)} %get-tuple-element.74.g1.mine), channel_id=1, source_target_pairs={{0,16},{16,0},{1,17},{17,1},{2,18},{18,2},{3,19},{19,3},{4,20},{20... | collective-permute-start | bytes 5406728 | tf_op jit(solution)/shard_map/ppermute | solution.py:1311
  31.8 16.1 %all-to-all-start.1 = ((bf16[8,336,128]{2,1,0:T(8,128)(2,1)}), bf16[8,336,128]{2,1,0:T(8,128)(2,1)S(1)}, u32[]{:S(2)}, u32[]{:S(2)}) async-start(bf16[8,336,128]{2,1,0:T(8,128)(2,1)} %merge.1.after), calls=%async_computation.1 | async-start | bytes 1376256 | tf_op jit(solution)/shard_map/all_to_all | solution.py:1315
  48.0 7.5 %collective-permute-start.3 = (bf16[368,128]{1,0:T(8,128)(2,1)S(1)}, bf16[368,128]{1,0:T(8,128)(2,1)S(1)}, u32[]{:S(2)}, u32[]{:S(2)}) collective-permute-start(bf16[368,128]{1,0:T(8,128)(2,1)S(1)} %cube.1.after.a), channel_id=1, source_target_pairs={{0,8},{1,9},{2,10},{3,11},{4,12},{5,13},{6,14},{7,15},{8,0},{9,1},... | collective-permute-start | bytes 282632 | tf_op jit(solution)/shard_map/ppermute | solution.py:1322
  55.5 7.5 %collective-permute-start.10 = (bf16[368,128]{1,0:T(8,128)(2,1)S(1)}, bf16[368,128]{1,0:T(8,128)(2,1)S(1)}, u32[]{:S(2)}, u32[]{:S(2)}) collective-permute-start(bf16[368,128]{1,0:T(8,128)(2,1)S(1)} %add.1.after.refs_0_), channel_id=1, source_target_pairs={{0,7},{1,6},{2,5},{3,4},{4,3},{5,2},{6,1},{7,0},{8,15},{9,14},{10,... | collective-permute-start | bytes 282632 | tf_op jit(solution)/shard_map/ppermute | solution.py:1322
  57.3 7.0 %collective-permute-start.9 = (bf16[368,128]{1,0:T(8,128)(2,1)S(1)}, bf16[368,128]{1,0:T(8,128)(2,1)S(1)}, u32[]{:S(2)}, u32[]{:S(2)}) collective-permute-start(bf16[368,128]{1,0:T(8,128)(2,1)S(1)} %add.1.after.refs_0_), channel_id=1, source_target_pairs={{0,6},{1,7},{2,4},{3,5},{4,2},{5,3},{6,0},{7,1},{8,14},{9,15},{10,... | collective-permute-start | bytes 282632 | tf_op jit(solution)/shard_map/ppermute | solution.py:1322
  58.6 9.7 %collective-permute-start.8 = (bf16[368,128]{1,0:T(8,128)(2,1)S(1)}, bf16[368,128]{1,0:T(8,128)(2,1)S(1)}, u32[]{:S(2)}, u32[]{:S(2)}) collective-permute-start(bf16[368,128]{1,0:T(8,128)(2,1)S(1)} %add.1.after.refs_0_), channel_id=1, source_target_pairs={{0,1},{1,0},{2,3},{3,2},{4,5},{5,4},{6,7},{7,6},{8,9},{9,8},{10,11... | collective-permute-start | bytes 282632 | tf_op jit(solution)/shard_map/ppermute | solution.py:1322
  60.0 8.3 %collective-permute-start.7 = (bf16[368,128]{1,0:T(8,128)(2,1)S(1)}, bf16[368,128]{1,0:T(8,128)(2,1)S(1)}, u32[]{:S(2)}, u32[]{:S(2)}) collective-permute-start(bf16[368,128]{1,0:T(8,128)(2,1)S(1)} %add.1.after.refs_0_), channel_id=1, source_target_pairs={{0,5},{1,4},{2,7},{3,6},{4,1},{5,0},{6,3},{7,2},{8,13},{9,12},{10,... | collective-permute-start | bytes 282632 | tf_op jit(solution)/shard_map/ppermute | solution.py:1322
  61.1 7.3 %collective-permute-start.6 = (bf16[368,128]{1,0:T(8,128)(2,1)S(1)}, bf16[368,128]{1,0:T(8,128)(2,1)S(1)}, u32[]{:S(2)}, u32[]{:S(2)}) collective-permute-start(bf16[368,128]{1,0:T(8,128)(2,1)S(1)} %add.1.after.refs_0_), channel_id=1, source_target_pairs={{0,2},{1,3},{2,0},{3,1},{4,6},{5,7},{6,4},{7,5},{8,10},{9,11},{10,... | collective-permute-start | bytes 282632 | tf_op jit(solution)/shard_map/ppermute | solution.py:1322
  63.0 5.5 %collective-permute-start.5 = (bf16[368,128]{1,0:T(8,128)(2,1)S(1)}, bf16[368,128]{1,0:T(8,128)(2,1)S(1)}, u32[]{:S(2)}, u32[]{:S(2)}) collective-permute-start(bf16[368,128]{1,0:T(8,128)(2,1)S(1)} %add.1.after.refs_0_), channel_id=1, source_target_pairs={{0,3},{1,2},{2,1},{3,0},{4,7},{5,6},{6,5},{7,4},{8,11},{9,10},{10,... | collective-permute-start | bytes 282632 | tf_op jit(solution)/shard_map/ppermute | solution.py:1322
  64.4 4.6 %collective-permute-start.4 = (bf16[368,128]{1,0:T(8,128)(2,1)S(1)}, bf16[368,128]{1,0:T(8,128)(2,1)S(1)}, u32[]{:S(2)}, u32[]{:S(2)}) collective-permute-start(bf16[368,128]{1,0:T(8,128)(2,1)S(1)} %add.1.after.refs_0_), channel_id=1, source_target_pairs={{0,4},{1,5},{2,6},{3,7},{4,0},{5,1},{6,2},{7,3},{8,12},{9,13},{10,... | collective-permute-start | bytes 282632 | tf_op jit(solution)/shard_map/ppermute | solution.py:1322
  69.1 1.8 %collective-permute-start.11 = (bf16[4,368,128]{2,1,0:T(8,128)(2,1)S(1)}, bf16[4,368,128]{2,1,0:T(8,128)(2,1)S(1)}, u32[]{:S(2)}, u32[]{:S(2)}) collective-permute-start(bf16[4,368,128]{2,1,0:T(8,128)(2,1)S(1)} %get-tuple-element.81.one.refs_0_), channel_id=1, source_target_pairs={{0,16},{16,0},{1,17},{17,1},{2,18},{18,2},{3,19},{19,3},{4,20},{20... | collective-permute-start | bytes 1130504 | tf_op jit(solution)/shard_map/ppermute | solution.py:1311
  69.1 2.2 %collective-permute-start.12 = (bf16[4,368,128]{2,1,0:T(8,128)(2,1)S(1)}, bf16[4,368,128]{2,1,0:T(8,128)(2,1)S(1)}, u32[]{:S(2)}, u32[]{:S(2)}) collective-permute-start(bf16[4,368,128]{2,1,0:T(8,128)(2,1)S(1)} %get-tuple-element.82.two.refs_1_), channel_id=1, source_target_pairs={{0,16},{16,0},{1,17},{17,1},{2,18},{18,2},{3,19},{19,3},{4,20},{20... | collective-permute-start | bytes 1130504 | tf_op jit(solution)/shard_map/ppermute | solution.py:1311

commit v3 on v2

--- a/solution.py
+++ b/solution.py
@@ -176,17 +176,18 @@
                 band[at : at + k1, :] = jnp.concatenate(pieces, axis=1).astype(BF16)
             edges.append(jnp.concatenate([line[:, 16:] for line in lines], axis=1))
         edge[...] = jnp.concatenate(edges, axis=0).astype(BF16)
-        tap, pix = iota((256, LANES), 0), iota((256, LANES), 1)
+        taps = w2t[...].astype(F32)
+        blank = jnp.zeros((k2, 2 * k1), F32)
         for half in range(2):
+            lines = [taps[:, 4 * k1 * (2 * half + u) : 4 * k1 * (2 * half + u + 1)] for u in range(2)]
+            pieces = (
+                [v for line in lines for v in (line[:, 2 * k1 :], blank)],
+                lines,
+                [v for line in lines for v in (blank, line[:, : 2 * k1])],
+            )
             for place in range(3):
-                hit = (
-                    ((tap & 15) == (pix & 15))
-                    & ((tap >> 6) == (pix >> 6) + 2 * half)
-                    & (((tap >> 4) & 3) == ((pix >> 4) & 3) + 2 - 2 * place)
-                )
                 at = (half * 3 + place) * k2
-                taps = dot(w2t[...], hit.astype(F32).astype(BF16))
-                band2[at : at + k2, :] = taps.astype(BF16)
+                band2[at : at + k2, :] = jnp.concatenate(pieces[place], axis=1).astype(BF16)
         bias1[...] = jnp.broadcast_to(column(table[AT_B1, 0:k1]), bias1.shape)
         bias2[...] = jnp.broadcast_to(column(table[AT_B2, 0:k2]), bias2.shape)
         held[...] = jnp.zeros_like(held)

time: 73.4 us -> 73.4 us (level)
  no operation moved by 1% of the time
where the time goes in v3:
time: 73.4 us; the launch traced here: 72.8 us
  Pallas kernels  40.8 us (56%)
  starting transfers between devices  26.1 us (36%)
  waiting for transfers between devices  4.27 us (6%)
  between operations  1.61 us (2%)
    all_to_all x2, starting transfers between devices, exchanged(): lax.all_to_all(value, 'batch', split_axis=0, concat_axis=0, axis_index_gr...  13.2 us
    ppermute x8, starting transfers between devices, partner(): lax.ppermute(value, 'batch', [(b, b ^ distance) for b in range(count)])  11.6 us
    pallas_call x1, Pallas kernels, first(): pl.pallas_call(functools.partial(first_kernel, draw=draw), in_specs=[SCAL...  9.49 us
    pallas_call x1, Pallas kernels, plan(): pl.pallas_call(functools.partial(plan_kernel, per_pair=per_pair, depth=de...  8.49 us
    pallas_call x1, Pallas kernels, encode(): pl.pallas_call(encode_kernel, in_specs=[SCALARS, ANYWHERE, near, near, AN...  7.54 us
    pallas_call x2, Pallas kernels, pixels(): pl.pallas_call(functools.partial(pixels_kernel, start=start), in_specs=[S...  7.47 us
    pallas_call x1, Pallas kernels, back(): pl.pallas_call(back_kernel, in_specs=[near] * 6, out_shape=(shape_of(*pad...  2.63 us
    all_to_all x2, waiting for transfers between devices, exchanged(): lax.all_to_all(value, 'batch', split_axis=0, concat_axis=0, axis_index_gr...  1.99 us
  transfers between devices with their start and end apart: 15, of which 7 were waited for; matrix products, arithmetic and copies ran while one was open for 0% of the time, Pallas kernels for 40%

profile of v3, /device:TPU:0, one launch (start us, length us, event | category | flops | bytes accessed | tf_op | source)
XLA Modules:
  0.0 72.8 jit_solution(4357712338543275337)
XLA Ops:
  1.3 1.6 %numbers.1 = (f32[256,128]{1,0:T(8,128)}, f32[32,128]{1,0:T(8,128)S(1)}) custom-call(s32[3,256]{1,0:T(4,128)} %options.1, s32[1,256]{1,0:T(1,128)} %bitcast.38, f32[3,3,256]{2,1,0:T(4,128)} %targets.1, s32[1,256]{1,0:T(1,128)} %bitcast.39, f32[1,16]{1,0:T(1,128)} %bitcast.40, f32[1,32]{1,0:T(1,128)} %bitcast.41, f32[1,128]{1,0:T(1,128)} %bitcast.42, ...), custom_call_target="tpu_custom_call" | custom-call | flops 1100000000 | bytes 3600000 | tf_op jit(solution)/shard_map/numbers/pallas_call | solution.py:1363
  2.9 8.3 %all-to-all-start = ((f32[16,16,128]{2,1,0:T(8,128)}), f32[16,16,128]{2,1,0:T(8,128)S(1)}, u32[]{:S(2)}, u32[]{:S(2)}) async-start(f32[16,16,128]{2,1,0:T(8,128)} %bitcast.12), calls=%async_computation | async-start | bytes 262144 | tf_op jit(solution)/shard_map/all_to_all | solution.py:1316
  11.2 7.5 %encode.1 = (bf16[21,20,16,128]{3,2,1,0:T(8,128)(2,1)}, bf16[21,20,16,128]{3,2,1,0:T(8,128)(2,1)}, bf16[2592,128]{1,0:T(8,128)(2,1)}, bf16[2592,128]{1,0:T(8,128...) custom-call(s32[1]{0:T(128)} %bitcast.section, bf16[84,84,4,256]{3,2,1,0:T(4,128)(2,1)} %bitcast.32, ...), custom_call_target="tpu_custom_call" | custom-call | flops 9900000256 | bytes 32400000 | tf_op jit(solution)/shard_map/encode/pallas_call | solution.py:1145
  19.0 8.5 %plan.1 = (bf16[2560,128]{1,0:T(8,128)(2,1)S(1)}, bf16[1280,128]{1,0:T(8,128)(2,1)S(1)}, bf16[1280,128]{1,0:T(8,128)(2,1)S(1)}, f32[32,128]{1,0:T(8,128)S(1)}, bf16[128,128]{1,0:T(8,128)(2,1)S(1)}) custom-call(s32[1]{0:T(128)} %bitcast.section, f32[256,128]{1,0:T(8,128)S(1)} %bitcast.30, bf16[128,128]{1,0:T(8,128)(2,1)S(1)} %get-tuple-element.61.enc, ...), custom_call_target="tpu_custom_call" | custom-call | flops 12099999744 | bytes 39600000 | tf_op jit(solution)/shard_map/plan/pallas_call | solution.py:1192
  27.6 0.5 collective-permute-start.1
  28.1 2.6 %back.1 = (bf16[22,20,16,128]{3,2,1,0:T(8,128)(2,1)S(1)}, f32[32,256]{1,0:T(8,128)S(1)}, f32[8,128]{1,0:T(8,128)S(1)}) custom-call(bf16[128,128]{1,0:T(8,128)(2,1)S(1)} %get-tuple-element.68.g3, bf16[2592,128]{1,0:T(8,128)(2,1)S(1)} %copy-done, bf16[2592,128]{1,0:T(8,128)(2,1)S(1)} %copy-done.3, bf16[21,20,16,128]{3,2,1,0:T(8,128)(2,1)S(1)} %copy-done.2, ...), custom_call_target="tpu_custom_call" | custom-call | flops 27499999232 | bytes 90000000 | tf_op jit(solution)/shard_map/back/pallas_call | solution.py:1224
  30.9 0.9 %merge.1.after = bf16[8,336,128]{2,1,0:T(8,128)(2,1)} custom-call(bf16[2560,128]{1,0:T(8,128)(2,1)S(1)} %get-tuple-element.64.keep, bf16[1280,128]{1,0:T(8,128)(2,1)S(1)} %collective-permute-done.recv_one, bf16[1280,128]{1,0:T(8,128)(2,1)S(1)} %collective-permute-done.1.recv_two, f32[32,128]{1,0:T(8,128)S(1)} %get-tuple-element.67.small, ...), custom_call_target="tpu_custom_call" | custom-call | flops 32999999488 | bytes 108000000 | tf_op jit(solution)/shard_map/merge/pallas_call | solution.py:1293
  31.8 4.8 %all-to-all-start.1 = ((bf16[8,336,128]{2,1,0:T(8,128)(2,1)}), bf16[8,336,128]{2,1,0:T(8,128)(2,1)S(1)}, u32[]{:S(2)}, u32[]{:S(2)}) async-start(bf16[8,336,128]{2,1,0:T(8,128)(2,1)} %merge.1.after), calls=%async_computation.1 | async-start | bytes 1376256 | tf_op jit(solution)/shard_map/all_to_all | solution.py:1316
  36.7 9.5 %first.1 = (bf16[32,128]{1,0:T(8,128)(2,1)S(1)}, f32[84,84,2,256]{3,2,1,0:T(2,128)}, bf16[288,256]{1,0:T(8,128)(2,1)S(1)}) custom-call(s32[1]{0:T(128)} %bitcast.section, bf16[84,84,4,256]{3,2,1,0:T(4,128)(2,1)} %bitcast.33, bf16[22,20,16,128]{3,2,1,0:T(8,128)(2,1)S(1)} %get-tuple-element.74.g1.mine, bf16[16,256]{1,0:T(8,128)(2,1)} %bitcast.37, ...), custom_call_target="tpu_custom_call" | custom-call | flops 49500000256 | bytes 162000000 | tf_op jit(solution)/shard_map/first/pallas_call | solution.py:1243
  46.2 1.8 %all-to-all-done.1.got = bf16[8,336,128]{2,1,0:T(8,128)(2,1)S(1)} async-done(((bf16[8,336,128]{2,1,0:T(8,128)(2,1)}), bf16[8,336,128]{2,1,0:T(8,128)(2,1)S(1)}, u32[]{:S(2)}, u32[]{:S(2)}) %all-to-all-start.1) | async-done | bytes 688160 | tf_op jit(solution)/shard_map/all_to_all | solution.py:1316
  48.0 2.4 %collective-permute-start.3 = (bf16[368,128]{1,0:T(8,128)(2,1)S(1)}, bf16[368,128]{1,0:T(8,128)(2,1)S(1)}, u32[]{:S(2)}, u32[]{:S(2)}) collective-permute-start(bf16[368,128]{1,0:T(8,128)(2,1)S(1)} %cube.1.after.a), channel_id=1, source_target_pairs={{0,8},{1,9},{2,10},{3,11},{4,12},{5,13},{6,14},{7,15},{8,0},{9,1},... | collective-permute-start | bytes 282632 | tf_op jit(solution)/shard_map/ppermute | solution.py:1323
  50.4 4.7 %pixels.2 = (f32[84,84,2,256]{3,2,1,0:T(2,128)}, f32[8,128]{1,0:T(8,128)S(1)}) custom-call(s32[1]{0:T(128)} %bitcast.section, bf16[288,256]{1,0:T(8,128)(2,1)S(1)} %get-tuple-element.76.band, bf16[22,20,16,128]{3,2,1,0:T(8,128)(2,1)S(1)} %get-tuple-element.74.g1.mine, ...), custom_call_target="tpu_custom_call", output_to_operand_aliasing={{0}: (5, {})} | custom-call | flops 4070000128 | bytes 13320000 | tf_op jit(solution)/shard_map/pixels/pallas_call | solution.py:1269
  55.5 1.8 %collective-permute-start.10 = (bf16[368,128]{1,0:T(8,128)(2,1)S(1)}, bf16[368,128]{1,0:T(8,128)(2,1)S(1)}, u32[]{:S(2)}, u32[]{:S(2)}) collective-permute-start(bf16[368,128]{1,0:T(8,128)(2,1)S(1)} %add.1.after.refs_0_), channel_id=1, source_target_pairs={{0,7},{1,6},{2,5},{3,4},{4,3},{5,2},{6,1},{7,0},{8,15},{9,14},{10,... | collective-permute-start | bytes 282632 | tf_op jit(solution)/shard_map/ppermute | solution.py:1323
  57.3 1.3 %collective-permute-start.9 = (bf16[368,128]{1,0:T(8,128)(2,1)S(1)}, bf16[368,128]{1,0:T(8,128)(2,1)S(1)}, u32[]{:S(2)}, u32[]{:S(2)}) collective-permute-start(bf16[368,128]{1,0:T(8,128)(2,1)S(1)} %add.1.after.refs_0_), channel_id=1, source_target_pairs={{0,6},{1,7},{2,4},{3,5},{4,2},{5,3},{6,0},{7,1},{8,14},{9,15},{10,... | collective-permute-start | bytes 282632 | tf_op jit(solution)/shard_map/ppermute | solution.py:1323
  58.6 1.4 %collective-permute-start.8 = (bf16[368,128]{1,0:T(8,128)(2,1)S(1)}, bf16[368,128]{1,0:T(8,128)(2,1)S(1)}, u32[]{:S(2)}, u32[]{:S(2)}) collective-permute-start(bf16[368,128]{1,0:T(8,128)(2,1)S(1)} %add.1.after.refs_0_), channel_id=1, source_target_pairs={{0,1},{1,0},{2,3},{3,2},{4,5},{5,4},{6,7},{7,6},{8,9},{9,8},{10,11... | collective-permute-start | bytes 282632 | tf_op jit(solution)/shard_map/ppermute | solution.py:1323
  60.0 1.1 %collective-permute-start.7 = (bf16[368,128]{1,0:T(8,128)(2,1)S(1)}, bf16[368,128]{1,0:T(8,128)(2,1)S(1)}, u32[]{:S(2)}, u32[]{:S(2)}) collective-permute-start(bf16[368,128]{1,0:T(8,128)(2,1)S(1)} %add.1.after.refs_0_), channel_id=1, source_target_pairs={{0,5},{1,4},{2,7},{3,6},{4,1},{5,0},{6,3},{7,2},{8,13},{9,12},{10,... | collective-permute-start | bytes 282632 | tf_op jit(solution)/shard_map/ppermute | solution.py:1323
  61.1 1.2 %collective-permute-start.6 = (bf16[368,128]{1,0:T(8,128)(2,1)S(1)}, bf16[368,128]{1,0:T(8,128)(2,1)S(1)}, u32[]{:S(2)}, u32[]{:S(2)}) collective-permute-start(bf16[368,128]{1,0:T(8,128)(2,1)S(1)} %add.1.after.refs_0_), channel_id=1, source_target_pairs={{0,2},{1,3},{2,0},{3,1},{4,6},{5,7},{6,4},{7,5},{8,10},{9,11},{10,... | collective-permute-start | bytes 282632 | tf_op jit(solution)/shard_map/ppermute | solution.py:1323
  62.3 0.8 %collective-permute-done.10.refs_7_ = bf16[368,128]{1,0:T(8,128)(2,1)S(1)} collective-permute-done((bf16[368,128]{1,0:T(8,128)(2,1)S(1)}, bf16[368,128]{1,0:T(8,128)(2,1)S(1)}, u32[]{:S(2)}, u32[]{:S(2)}) %collective-permute-start.10) | collective-permute-done | bytes 94240 | tf_op jit(solution)/shard_map/ppermute | solution.py:1323
  63.0 1.4 %collective-permute-start.5 = (bf16[368,128]{1,0:T(8,128)(2,1)S(1)}, bf16[368,128]{1,0:T(8,128)(2,1)S(1)}, u32[]{:S(2)}, u32[]{:S(2)}) collective-permute-start(bf16[368,128]{1,0:T(8,128)(2,1)S(1)} %add.1.after.refs_0_), channel_id=1, source_target_pairs={{0,3},{1,2},{2,1},{3,0},{4,7},{5,6},{6,5},{7,4},{8,11},{9,10},{10,... | collective-permute-start | bytes 282632 | tf_op jit(solution)/shard_map/ppermute | solution.py:1323
  64.4 1.1 %collective-permute-start.4 = (bf16[368,128]{1,0:T(8,128)(2,1)S(1)}, bf16[368,128]{1,0:T(8,128)(2,1)S(1)}, u32[]{:S(2)}, u32[]{:S(2)}) collective-permute-start(bf16[368,128]{1,0:T(8,128)(2,1)S(1)} %add.1.after.refs_0_), channel_id=1, source_target_pairs={{0,4},{1,5},{2,6},{3,7},{4,0},{5,1},{6,2},{7,3},{8,12},{9,13},{10,... | collective-permute-start | bytes 282632 | tf_op jit(solution)/shard_map/ppermute | solution.py:1323
  65.5 2.8 %pixels.3 = (f32[84,84,2,256]{3,2,1,0:T(2,128)}, f32[8,128]{1,0:T(8,128)S(1)}) custom-call(s32[1]{0:T(128)} %bitcast.section, bf16[288,256]{1,0:T(8,128)(2,1)S(1)} %get-tuple-element.76.band, bf16[22,20,16,128]{3,2,1,0:T(8,128)(2,1)S(1)} %get-tuple-element.74.g1.mine, ...), custom_call_target="tpu_custom_call", output_to_operand_aliasing={{0}: (5, {})} | custom-call | flops 2090000000 | bytes 6840000 | tf_op jit(solution)/shard_map/pixels/pallas_call | solution.py:1269
  69.2 0.5 collective-permute-start.12
  69.7 1.2 %own.1 = (f32[2592,128]{1,0:T(8,128)}, f32[18,128,128]{2,1,0:T(8,128)}, f32[128,128]{1,0:T(8,128)}) custom-call(s32[1]{0:T(128)} %bitcast.section, bf16[4,368,128]{2,1,0:T(8,128)(2,1)S(1)} %get-tuple-element.81.one.refs_0_, bf16[4,368,128]{2,1,0:T(8,128)(2,1)S(1)} %get-tuple-element.82.two.refs_1_), custom_call_target="tpu_custom_call" | custom-call | flops 1100000000 | bytes 3600000 | tf_op jit(solution)/shard_map/own/pallas_call | solution.py:1445
  71.4 1.3 %unpack.1 = (f32[2592,128]{1,0:T(8,128)}, f32[18,128,128]{2,1,0:T(8,128)}, f32[128,128]{1,0:T(8,128)}, f32[1,1]{1,0:T(1,128)}, f32[16,256]{1,0:T(8,128)}, /*inde...) custom-call(s32[1]{0:T(128)} %bitcast.section, ...), custom_call_target="tpu_custom_call", output_to_operand_aliasing={{0}: (5, {}), {1}: (6, {}), {2}: (7, {})} | custom-call | flops 1650000000 | bytes 5400000 | tf_op jit(solution)/shard_map/unpack/pallas_call | solution.py:1455
  (27 shorter events, 2.3 us)
Async XLA Ops:
  2.9 16.1 %all-to-all-start = ((f32[16,16,128]{2,1,0:T(8,128)}), f32[16,16,128]{2,1,0:T(8,128)S(1)}, u32[]{:S(2)}, u32[]{:S(2)}) async-start(f32[16,16,128]{2,1,0:T(8,128)} %bitcast.12), calls=%async_computation | async-start | bytes 262144 | tf_op jit(solution)/shard_map/all_to_all | solution.py:1316
  19.0 9.1 %copy-start = (bf16[2592,128]{1,0:T(8,128)(2,1)S(1)}, bf16[2592,128]{1,0:T(8,128)(2,1)}, u32[]{:S(2)}) copy-start(bf16[2592,128]{1,0:T(8,128)(2,1)} %lw.1) | copy-start | bytes 1990660
  19.0 9.1 %copy-start.1 = (bf16[21,20,16,128]{3,2,1,0:T(8,128)(2,1)S(1)}, bf16[21,20,16,128]{3,2,1,0:T(8,128)(2,1)}, u32[]{:S(2)}) copy-start(bf16[21,20,16,128]{3,2,1,0:T(8,128)(2,1)} %get-tuple-element.71.h1) | copy-start | bytes 5160964
  19.0 9.1 %copy-start.2 = (bf16[21,20,16,128]{3,2,1,0:T(8,128)(2,1)S(1)}, bf16[21,20,16,128]{3,2,1,0:T(8,128)(2,1)}, u32[]{:S(2)}) copy-start(bf16[21,20,16,128]{3,2,1,0:T(8,128)(2,1)} %get-tuple-element.70.s1) | copy-start | bytes 5160964
  19.0 9.1 %copy-start.3 = (bf16[2592,128]{1,0:T(8,128)(2,1)S(1)}, bf16[2592,128]{1,0:T(8,128)(2,1)}, u32[]{:S(2)}) copy-start(bf16[2592,128]{1,0:T(8,128)(2,1)} %get-tuple-element.69.s2) | copy-start | bytes 1990660
  27.5 3.4 %collective-permute-start = (bf16[1280,128]{1,0:T(8,128)(2,1)S(1)}, bf16[1280,128]{1,0:T(8,128)(2,1)S(1)}, u32[]{:S(2)}, u32[]{:S(2)}) collective-permute-start(bf16[1280,128]{1,0:T(8,128)(2,1)S(1)} %get-tuple-element.65), channel_id=1, source_target_pairs={{0,16},{16,0},{1,17},{17,1},{2,18},{18,2},{3,19},{19,3},{4,20},{20... | collective-permute-start | bytes 983048 | tf_op jit(solution)/shard_map/ppermute | solution.py:1312
  27.6 3.3 %collective-permute-start.1 = (bf16[1280,128]{1,0:T(8,128)(2,1)S(1)}, bf16[1280,128]{1,0:T(8,128)(2,1)S(1)}, u32[]{:S(2)}, u32[]{:S(2)}) collective-permute-start(bf16[1280,128]{1,0:T(8,128)(2,1)S(1)} %get-tuple-element.66), channel_id=1, source_target_pairs={{0,16},{16,0},{1,17},{17,1},{2,18},{18,2},{3,19},{19,3},{4,20},{20... | collective-permute-start | bytes 983048 | tf_op jit(solution)/shard_map/ppermute | solution.py:1312
  30.7 5.9 %collective-permute-start.2 = (bf16[22,20,16,128]{3,2,1,0:T(8,128)(2,1)S(1)}, bf16[22,20,16,128]{3,2,1,0:T(8,128)(2,1)}, u32[]{:S(2)}, u32[]{:S(2)}) collective-permute-start(bf16[22,20,16,128]{3,2,1,0:T(8,128)(2,1)S(1)} %get-tuple-element.74.g1.mine), channel_id=1, source_target_pairs={{0,16},{16,0},{1,17},{17,1},{2,18},{18,2},{3,19},{19,3},{4,20},{20... | collective-permute-start | bytes 5406728 | tf_op jit(solution)/shard_map/ppermute | solution.py:1312
  31.8 16.1 %all-to-all-start.1 = ((bf16[8,336,128]{2,1,0:T(8,128)(2,1)}), bf16[8,336,128]{2,1,0:T(8,128)(2,1)S(1)}, u32[]{:S(2)}, u32[]{:S(2)}) async-start(bf16[8,336,128]{2,1,0:T(8,128)(2,1)} %merge.1.after), calls=%async_computation.1 | async-start | bytes 1376256 | tf_op jit(solution)/shard_map/all_to_all | solution.py:1316
  48.0 7.5 %collective-permute-start.3 = (bf16[368,128]{1,0:T(8,128)(2,1)S(1)}, bf16[368,128]{1,0:T(8,128)(2,1)S(1)}, u32[]{:S(2)}, u32[]{:S(2)}) collective-permute-start(bf16[368,128]{1,0:T(8,128)(2,1)S(1)} %cube.1.after.a), channel_id=1, source_target_pairs={{0,8},{1,9},{2,10},{3,11},{4,12},{5,13},{6,14},{7,15},{8,0},{9,1},... | collective-permute-start | bytes 282632 | tf_op jit(solution)/shard_map/ppermute | solution.py:1323
  55.5 7.5 %collective-permute-start.10 = (bf16[368,128]{1,0:T(8,128)(2,1)S(1)}, bf16[368,128]{1,0:T(8,128)(2,1)S(1)}, u32[]{:S(2)}, u32[]{:S(2)}) collective-permute-start(bf16[368,128]{1,0:T(8,128)(2,1)S(1)} %add.1.after.refs_0_), channel_id=1, source_target_pairs={{0,7},{1,6},{2,5},{3,4},{4,3},{5,2},{6,1},{7,0},{8,15},{9,14},{10,... | collective-permute-start | bytes 282632 | tf_op jit(solution)/shard_map/ppermute | solution.py:1323
  57.3 7.1 %collective-permute-start.9 = (bf16[368,128]{1,0:T(8,128)(2,1)S(1)}, bf16[368,128]{1,0:T(8,128)(2,1)S(1)}, u32[]{:S(2)}, u32[]{:S(2)}) collective-permute-start(bf16[368,128]{1,0:T(8,128)(2,1)S(1)} %add.1.after.refs_0_), channel_id=1, source_target_pairs={{0,6},{1,7},{2,4},{3,5},{4,2},{5,3},{6,0},{7,1},{8,14},{9,15},{10,... | collective-permute-start | bytes 282632 | tf_op jit(solution)/shard_map/ppermute | solution.py:1323
  58.6 9.7 %collective-permute-start.8 = (bf16[368,128]{1,0:T(8,128)(2,1)S(1)}, bf16[368,128]{1,0:T(8,128)(2,1)S(1)}, u32[]{:S(2)}, u32[]{:S(2)}) collective-permute-start(bf16[368,128]{1,0:T(8,128)(2,1)S(1)} %add.1.after.refs_0_), channel_id=1, source_target_pairs={{0,1},{1,0},{2,3},{3,2},{4,5},{5,4},{6,7},{7,6},{8,9},{9,8},{10,11... | collective-permute-start | bytes 282632 | tf_op jit(solution)/shard_map/ppermute | solution.py:1323
  60.0 8.3 %collective-permute-start.7 = (bf16[368,128]{1,0:T(8,128)(2,1)S(1)}, bf16[368,128]{1,0:T(8,128)(2,1)S(1)}, u32[]{:S(2)}, u32[]{:S(2)}) collective-permute-start(bf16[368,128]{1,0:T(8,128)(2,1)S(1)} %add.1.after.refs_0_), channel_id=1, source_target_pairs={{0,5},{1,4},{2,7},{3,6},{4,1},{5,0},{6,3},{7,2},{8,13},{9,12},{10,... | collective-permute-start | bytes 282632 | tf_op jit(solution)/shard_map/ppermute | solution.py:1323
  61.1 7.2 %collective-permute-start.6 = (bf16[368,128]{1,0:T(8,128)(2,1)S(1)}, bf16[368,128]{1,0:T(8,128)(2,1)S(1)}, u32[]{:S(2)}, u32[]{:S(2)}) collective-permute-start(bf16[368,128]{1,0:T(8,128)(2,1)S(1)} %add.1.after.refs_0_), channel_id=1, source_target_pairs={{0,2},{1,3},{2,0},{3,1},{4,6},{5,7},{6,4},{7,5},{8,10},{9,11},{10,... | collective-permute-start | bytes 282632 | tf_op jit(solution)/shard_map/ppermute | solution.py:1323
  63.0 5.5 %collective-permute-start.5 = (bf16[368,128]{1,0:T(8,128)(2,1)S(1)}, bf16[368,128]{1,0:T(8,128)(2,1)S(1)}, u32[]{:S(2)}, u32[]{:S(2)}) collective-permute-start(bf16[368,128]{1,0:T(8,128)(2,1)S(1)} %add.1.after.refs_0_), channel_id=1, source_target_pairs={{0,3},{1,2},{2,1},{3,0},{4,7},{5,6},{6,5},{7,4},{8,11},{9,10},{10,... | collective-permute-start | bytes 282632 | tf_op jit(solution)/shard_map/ppermute | solution.py:1323
  64.4 4.6 %collective-permute-start.4 = (bf16[368,128]{1,0:T(8,128)(2,1)S(1)}, bf16[368,128]{1,0:T(8,128)(2,1)S(1)}, u32[]{:S(2)}, u32[]{:S(2)}) collective-permute-start(bf16[368,128]{1,0:T(8,128)(2,1)S(1)} %add.1.after.refs_0_), channel_id=1, source_target_pairs={{0,4},{1,5},{2,6},{3,7},{4,0},{5,1},{6,2},{7,3},{8,12},{9,13},{10,... | collective-permute-start | bytes 282632 | tf_op jit(solution)/shard_map/ppermute | solution.py:1323
  69.1 1.8 %collective-permute-start.11 = (bf16[4,368,128]{2,1,0:T(8,128)(2,1)S(1)}, bf16[4,368,128]{2,1,0:T(8,128)(2,1)S(1)}, u32[]{:S(2)}, u32[]{:S(2)}) collective-permute-start(bf16[4,368,128]{2,1,0:T(8,128)(2,1)S(1)} %get-tuple-element.81.one.refs_0_), channel_id=1, source_target_pairs={{0,16},{16,0},{1,17},{17,1},{2,18},{18,2},{3,19},{19,3},{4,20},{20... | collective-permute-start | bytes 1130504 | tf_op jit(solution)/shard_map/ppermute | solution.py:1312
  69.2 2.2 %collective-permute-start.12 = (bf16[4,368,128]{2,1,0:T(8,128)(2,1)S(1)}, bf16[4,368,128]{2,1,0:T(8,128)(2,1)S(1)}, u32[]{:S(2)}, u32[]{:S(2)}) collective-permute-start(bf16[4,368,128]{2,1,0:T(8,128)(2,1)S(1)} %get-tuple-element.82.two.refs_1_), channel_id=1, source_target_pairs={{0,16},{16,0},{1,17},{17,1},{2,18},{18,2},{3,19},{19,3},{4,20},{20... | collective-permute-start | bytes 1130504 | tf_op jit(solution)/shard_map/ppermute | solution.py:1312
